TPU v7x, 128 devices: a whole 4x4x4 slice. The times are simulated.
128 devices in a mesh: blk: 16 (over y, x_hi, core), rows: 8 (over x_lo, z).
Axes of the slice: x: 4 (x_hi: 2, x_lo: 2; x = x_hi * 2 + x_lo), y: 4, z: 4, core: 2. Of those that a mesh axis runs over, the one named last changes fastest.
Arguments:
- observation_points: bfloat16 [98304, 32], P(('blk', 'rows')), may hold values from -6 to 6
- search_vectors: float32 [98304, 16], P(('blk', 'rows')), may hold values from -3 to 3
- shrinkage_levels: float32 [16], replicated, may hold values from 0.1 to 10
- holdout_group: int32 [98304, 1], P(('blk', 'rows')), may hold values from 0 to 511; in each aligned block of 768 rows (0 to 767, 768 to 1535, ...) at most 3 rows name the same one
Outputs:
- mapped_search_output: float32 [98304, 16], P(('blk', 'rows'))
- fold_curv: float32 [512, 256], P(('blk', 'rows'))
Inputs may be any that keep to these rules, and one draw needn't show every extreme that they name: `holdout_group`: among the rows of one device (aligned blocks of 768 rows) no fold appears more than 3 times, and some fold appears exactly 3 times; every fold appears somewhere.
All inputs are finite; a program needn't handle non-finite values.
Results may differ from a plain program's by a relative error of at most 0.0008.
Values may be sent and summed in bfloat16 or wider, within the bound.
No kernel may reach another device: no remote copies, remote signals or barrier semaphores. Data moves between devices by JAX's collectives and lax.ppermute only.
A program may use at most 128 MiB of HBM per device.

v0:
```python
import jax
import jax.numpy as jnp
from jax import lax
from jax.sharding import PartitionSpec as P

FOLD_DEV = 4


kernel_rate = 0.5
element_room = 6 * 1024 * 1024


def kernel_apply(queries, query_norms, columns, coeffs):
    inner_prod = jnp.einsum("qf,pf->qp", queries, columns, preferred_element_type=jnp.float32)
    wide_cols = columns.astype(jnp.float32)
    col_norms = jnp.sum(wide_cols * wide_cols, axis=1)
    distance = query_norms[:, None] + col_norms[None, :] - 2.0 * inner_prod
    weights = jnp.exp(-kernel_rate * distance).astype(jnp.bfloat16)
    return jnp.dot(weights, coeffs, preferred_element_type=jnp.float32)


def block_width(span_rows, query_count):
    limit = max(512, element_room // max(query_count, 1))
    best = 1
    for factor in range(1, limit + 1):
        if span_rows % factor == 0:
            best = factor
    return best


def fold_in_pieces(running, pieces, queries, query_norms):
    columns, coeffs = pieces
    span_rows = columns.shape[0]
    col_block = block_width(span_rows, queries.shape[0])
    if col_block == span_rows:
        return kernel_apply(queries, query_norms, columns, coeffs)
    col_blocks = columns.reshape(span_rows // col_block, col_block, columns.shape[1])
    coeff_blocks = coeffs.reshape(span_rows // col_block, col_block, coeffs.shape[1])

    def add_block(running_total_sum, block_pair):
        return (
            running_total_sum + kernel_apply(queries, query_norms, block_pair[0], block_pair[1]),
            0,
        )

    scanned = lax.scan(add_block, running, (col_blocks, coeff_blocks))
    return scanned[0]


def body(observation_points, search_vectors, shrinkage_levels, holdout_group):
    half_dirs = search_vectors.astype(jnp.bfloat16)
    local_rows = observation_points.shape[0]
    pen_count = search_vectors.shape[1]
    panel_x, panel_v = (
        lax.all_gather(observation_points, "rows", axis=0, tiled=True),
        lax.all_gather(half_dirs, "rows", axis=0, tiled=True),
    )
    wide_q = observation_points.astype(jnp.float32)
    query_norms = jnp.sum(wide_q * wide_q, axis=1)
    gram_share = fold_in_pieces(
        jnp.zeros((local_rows, pen_count), jnp.float32),
        (
            lax.all_gather(panel_x, "blk", axis=0, tiled=True),
            lax.all_gather(panel_v, "blk", axis=0, tiled=True),
        ),
        observation_points,
        query_norms,
    )
    mapped_search_output = gram_share + shrinkage_levels[None, :] * search_vectors
    blk_count = lax.axis_size("blk")
    row_count = lax.axis_size("rows")
    devices = blk_count * row_count
    fold_count = FOLD_DEV * devices
    slot_count = max(2, 2 * local_rows // fold_count)
    fold_scale = FOLD_DEV / local_rows
    fold_ids = holdout_group[:, 0]
    row_iota = lax.broadcasted_iota(jnp.int32, (local_rows, local_rows), 0)
    col_iota = lax.broadcasted_iota(jnp.int32, (local_rows, local_rows), 1)
    earlier = (fold_ids[:, None] == fold_ids[None, :]) & (col_iota < row_iota)
    slot_rank = jnp.sum(earlier.astype(jnp.int32), axis=1)
    position = fold_ids * slot_count + slot_rank
    rows_out = jnp.concatenate([search_vectors, mapped_search_output], axis=1)
    buffer = (
        jnp.zeros((fold_count * slot_count, 2 * pen_count), jnp.float32).at[position].set(rows_out)
    )
    flat_len = FOLD_DEV * slot_count * 2 * pen_count
    received = lax.all_to_all(
        buffer.reshape(devices, flat_len), ("blk", "rows"), split_axis=0, concat_axis=0, tiled=True
    )
    received = received.reshape(devices, FOLD_DEV, slot_count, 2, pen_count)
    per_fold_sums = jnp.einsum(
        "sgma,sgmb->gab",
        received[:, :, :, 0],
        received[:, :, :, 1],
        precision=lax.Precision.HIGHEST,
        preferred_element_type=jnp.float32,
    ).reshape(FOLD_DEV, pen_count * pen_count)
    return (mapped_search_output, per_fold_sums * fold_scale)


def solution(mesh):
    placed = (P(("blk", "rows"), None), P(("blk", "rows"), None), P(), P(("blk", "rows"), None))
    return jax.shard_map(
        body,
        mesh=mesh,
        in_specs=placed,
        out_specs=(P(("blk", "rows"), None), P(("blk", "rows"), None)),
        check_vma=False,
    )
```

profile of v0, /device:TPU:1, one launch (start us, length us, event | category | flops | bytes accessed | tf_op | source)
XLA Modules:
  0.0 336.5 jit_solution(18393252318444904209)
XLA Ops:
  8.0 26.1 %all_gather.14 = bf16[6144,16]{0,1:T(8,128)(2,1)} all-gather(bf16[768,16]{0,1:T(8,128)(2,1)S(1)} %convert_element_type.16), channel_id=1, replica_groups=mesh['blk'=16,'rows'=8] {'rows'}, dimensions={0}, use_global_device_ids=true | all-gather | bytes 221184 | tf_op jit(solution)/shard_map/all_gather | solution.py:56
  34.2 25.1 %all_gather.12 = bf16[6144,32]{0,1:T(8,128)(2,1)} all-gather(bf16[768,32]{0,1:T(8,128)(2,1)} %param.6), channel_id=1, replica_groups=mesh['blk'=16,'rows'=8] {'rows'}, dimensions={0}, use_global_device_ids=true | all-gather | bytes 442368 | tf_op jit(solution)/shard_map/all_gather | solution.py:55
  61.8 31.2 %all-gather.5.cloned.1.call-done = bf16[98304,16]{0,1:T(8,128)(2,1)} async-done(((bf16[6144,16]{0,1:T(8,128)(2,1)}), bf16[98304,16]{0,1:T(8,128)(2,1)}) %all-gather.5.cloned.1.call-update) | async-done | bytes 3145744 | tf_op jit(solution)/shard_map/all_gather | solution.py:64
  95.1 63.3 %all-gather.3.cloned.1.call-done = bf16[98304,32]{0,1:T(8,128)(2,1)} async-done(((bf16[6144,32]{0,1:T(8,128)(2,1)}), bf16[98304,32]{0,1:T(8,128)(2,1)}) %all-gather.3.cloned.1.call-update) | async-done | bytes 6291472 | tf_op jit(solution)/shard_map/all_gather | solution.py:63
  158.4 19.6 %copy.20 = bf16[98304,32]{1,0:T(8,128)(2,1)} copy(bf16[98304,32]{0,1:T(8,128)(2,1)} %all-gather.3.cloned.1.call-done) | data formatting | bytes 12582912 | tf_op jit(solution)/shard_map/all_gather | solution.py:63
  178.1 129.3 %while.11 = (s32[]{:T(128)}, f32[768,16]{0,1:T(8,128)S(1)}, f32[768]{0:T(1024)S(1)}, bf16[12,8192,32]{2,1,0:T(8,128)(2,1)}, bf16[768,32]{0,1:T(8,128)(2,1)S(1)},...) while((s32[]{:T(128)}, f32[768,16]{0,1:T(8,128)S(1)}, f32[768]{0:T(1024)S(1)}, ...), condition=%wide.region_3.4_spmd.clone, body=%wide.region_1.3_spmd.clone.sunk | while | flops 636239872 | bytes 3101795 | solution.py:46
  178.1 2.8 multiply_reduce_fusion.3
  180.8 8.0 %fusion.34 = f32[768,16]{0,1:T(8,128)S(1)} fusion(bf16[768,32]{0,1:T(8,128)(2,1)S(1)} %get-tuple-element.143, f32[8192]{0:T(1024)S(1)} %multiply_reduce_fusion.3, f32[768]{0:T(1024)S(1)} %get-tuple-element.141, bf16[12,8192,32]{2,1,0:T(8,128)(2,1)} %get-tuple-element.142, s32[]{:T(128)} %get-tuple-element.131, ...), kind=kOutput, calls=%fused_computation.13.clone.1 | convolution fusion | flops 635461632 | bytes 2544641 | tf_op jit(solution)/shard_map/while/body/eval_jaxpr/dot_general | solution.py:19
  188.9 2.8 multiply_reduce_fusion.3
  191.6 8.0 %fusion.34 = f32[768,16]{0,1:T(8,128)S(1)} fusion(bf16[768,32]{0,1:T(8,128)(2,1)S(1)} %get-tuple-element.143, f32[8192]{0:T(1024)S(1)} %multiply_reduce_fusion.3, f32[768]{0:T(1024)S(1)} %get-tuple-element.141, bf16[12,8192,32]{2,1,0:T(8,128)(2,1)} %get-tuple-element.142, s32[]{:T(128)} %get-tuple-element.131, ...), kind=kOutput, calls=%fused_computation.13.clone.1 | convolution fusion | flops 635461632 | bytes 2544641 | tf_op jit(solution)/shard_map/while/body/eval_jaxpr/dot_general | solution.py:19
  199.6 2.8 multiply_reduce_fusion.3
  202.4 8.0 %fusion.34 = f32[768,16]{0,1:T(8,128)S(1)} fusion(bf16[768,32]{0,1:T(8,128)(2,1)S(1)} %get-tuple-element.143, f32[8192]{0:T(1024)S(1)} %multiply_reduce_fusion.3, f32[768]{0:T(1024)S(1)} %get-tuple-element.141, bf16[12,8192,32]{2,1,0:T(8,128)(2,1)} %get-tuple-element.142, s32[]{:T(128)} %get-tuple-element.131, ...), kind=kOutput, calls=%fused_computation.13.clone.1 | convolution fusion | flops 635461632 | bytes 2544641 | tf_op jit(solution)/shard_map/while/body/eval_jaxpr/dot_general | solution.py:19
  210.4 2.8 multiply_reduce_fusion.3
  213.2 8.0 %fusion.34 = f32[768,16]{0,1:T(8,128)S(1)} fusion(bf16[768,32]{0,1:T(8,128)(2,1)S(1)} %get-tuple-element.143, f32[8192]{0:T(1024)S(1)} %multiply_reduce_fusion.3, f32[768]{0:T(1024)S(1)} %get-tuple-element.141, bf16[12,8192,32]{2,1,0:T(8,128)(2,1)} %get-tuple-element.142, s32[]{:T(128)} %get-tuple-element.131, ...), kind=kOutput, calls=%fused_computation.13.clone.1 | convolution fusion | flops 635461632 | bytes 2544641 | tf_op jit(solution)/shard_map/while/body/eval_jaxpr/dot_general | solution.py:19
  221.2 2.8 multiply_reduce_fusion.3
  223.9 8.0 %fusion.34 = f32[768,16]{0,1:T(8,128)S(1)} fusion(bf16[768,32]{0,1:T(8,128)(2,1)S(1)} %get-tuple-element.143, f32[8192]{0:T(1024)S(1)} %multiply_reduce_fusion.3, f32[768]{0:T(1024)S(1)} %get-tuple-element.141, bf16[12,8192,32]{2,1,0:T(8,128)(2,1)} %get-tuple-element.142, s32[]{:T(128)} %get-tuple-element.131, ...), kind=kOutput, calls=%fused_computation.13.clone.1 | convolution fusion | flops 635461632 | bytes 2544641 | tf_op jit(solution)/shard_map/while/body/eval_jaxpr/dot_general | solution.py:19
  232.0 2.8 multiply_reduce_fusion.3
  234.7 8.0 %fusion.34 = f32[768,16]{0,1:T(8,128)S(1)} fusion(bf16[768,32]{0,1:T(8,128)(2,1)S(1)} %get-tuple-element.143, f32[8192]{0:T(1024)S(1)} %multiply_reduce_fusion.3, f32[768]{0:T(1024)S(1)} %get-tuple-element.141, bf16[12,8192,32]{2,1,0:T(8,128)(2,1)} %get-tuple-element.142, s32[]{:T(128)} %get-tuple-element.131, ...), kind=kOutput, calls=%fused_computation.13.clone.1 | convolution fusion | flops 635461632 | bytes 2544641 | tf_op jit(solution)/shard_map/while/body/eval_jaxpr/dot_general | solution.py:19
  242.7 2.8 multiply_reduce_fusion.3
  245.5 8.0 %fusion.34 = f32[768,16]{0,1:T(8,128)S(1)} fusion(bf16[768,32]{0,1:T(8,128)(2,1)S(1)} %get-tuple-element.143, f32[8192]{0:T(1024)S(1)} %multiply_reduce_fusion.3, f32[768]{0:T(1024)S(1)} %get-tuple-element.141, bf16[12,8192,32]{2,1,0:T(8,128)(2,1)} %get-tuple-element.142, s32[]{:T(128)} %get-tuple-element.131, ...), kind=kOutput, calls=%fused_computation.13.clone.1 | convolution fusion | flops 635461632 | bytes 2544641 | tf_op jit(solution)/shard_map/while/body/eval_jaxpr/dot_general | solution.py:19
  253.5 2.8 multiply_reduce_fusion.3
  256.3 8.0 %fusion.34 = f32[768,16]{0,1:T(8,128)S(1)} fusion(bf16[768,32]{0,1:T(8,128)(2,1)S(1)} %get-tuple-element.143, f32[8192]{0:T(1024)S(1)} %multiply_reduce_fusion.3, f32[768]{0:T(1024)S(1)} %get-tuple-element.141, bf16[12,8192,32]{2,1,0:T(8,128)(2,1)} %get-tuple-element.142, s32[]{:T(128)} %get-tuple-element.131, ...), kind=kOutput, calls=%fused_computation.13.clone.1 | convolution fusion | flops 635461632 | bytes 2544641 | tf_op jit(solution)/shard_map/while/body/eval_jaxpr/dot_general | solution.py:19
  264.3 2.8 multiply_reduce_fusion.3
  267.0 8.0 %fusion.34 = f32[768,16]{0,1:T(8,128)S(1)} fusion(bf16[768,32]{0,1:T(8,128)(2,1)S(1)} %get-tuple-element.143, f32[8192]{0:T(1024)S(1)} %multiply_reduce_fusion.3, f32[768]{0:T(1024)S(1)} %get-tuple-element.141, bf16[12,8192,32]{2,1,0:T(8,128)(2,1)} %get-tuple-element.142, s32[]{:T(128)} %get-tuple-element.131, ...), kind=kOutput, calls=%fused_computation.13.clone.1 | convolution fusion | flops 635461632 | bytes 2544641 | tf_op jit(solution)/shard_map/while/body/eval_jaxpr/dot_general | solution.py:19
  275.1 2.8 multiply_reduce_fusion.3
  277.8 8.0 %fusion.34 = f32[768,16]{0,1:T(8,128)S(1)} fusion(bf16[768,32]{0,1:T(8,128)(2,1)S(1)} %get-tuple-element.143, f32[8192]{0:T(1024)S(1)} %multiply_reduce_fusion.3, f32[768]{0:T(1024)S(1)} %get-tuple-element.141, bf16[12,8192,32]{2,1,0:T(8,128)(2,1)} %get-tuple-element.142, s32[]{:T(128)} %get-tuple-element.131, ...), kind=kOutput, calls=%fused_computation.13.clone.1 | convolution fusion | flops 635461632 | bytes 2544641 | tf_op jit(solution)/shard_map/while/body/eval_jaxpr/dot_general | solution.py:19
  285.8 2.8 multiply_reduce_fusion.3
  288.6 8.0 %fusion.34 = f32[768,16]{0,1:T(8,128)S(1)} fusion(bf16[768,32]{0,1:T(8,128)(2,1)S(1)} %get-tuple-element.143, f32[8192]{0:T(1024)S(1)} %multiply_reduce_fusion.3, f32[768]{0:T(1024)S(1)} %get-tuple-element.141, bf16[12,8192,32]{2,1,0:T(8,128)(2,1)} %get-tuple-element.142, s32[]{:T(128)} %get-tuple-element.131, ...), kind=kOutput, calls=%fused_computation.13.clone.1 | convolution fusion | flops 635461632 | bytes 2544641 | tf_op jit(solution)/shard_map/while/body/eval_jaxpr/dot_general | solution.py:19
  296.6 2.8 multiply_reduce_fusion.3
  299.4 8.0 %fusion.34 = f32[768,16]{0,1:T(8,128)S(1)} fusion(bf16[768,32]{0,1:T(8,128)(2,1)S(1)} %get-tuple-element.143, f32[8192]{0:T(1024)S(1)} %multiply_reduce_fusion.3, f32[768]{0:T(1024)S(1)} %get-tuple-element.141, bf16[12,8192,32]{2,1,0:T(8,128)(2,1)} %get-tuple-element.142, s32[]{:T(128)} %get-tuple-element.131, ...), kind=kOutput, calls=%fused_computation.13.clone.1 | convolution fusion | flops 635461632 | bytes 2544641 | tf_op jit(solution)/shard_map/while/body/eval_jaxpr/dot_general | solution.py:19
  307.6 4.4 %scatter_custom_fusion = f32[1536,32]{1,0:T(8,128)S(1)} fusion(s32[768]{0:T(1024)S(1)} %fusion.25, f32[768,32]{1,0:T(8,128)S(1)} %copy.22, f32[]{:T(128)} %constant.4.clone.1), kind=kCustom, calls=%fused_computation.25 | custom fusion | bytes 196612 | tf_op jit(solution)/shard_map/scatter | solution.py:84
  312.4 16.2 %all_to_all.10 = f32[128,1,384]{2,1,0:T(1,128)S(1)} all-to-all(f32[128,1,384]{2,1,0:T(1,128)S(1)} %all_to_all.8), channel_id=1, replica_groups=mesh['blk'=16,'rows'=8] {'blk','rows'}, dimensions={0} | all-to-all | bytes 393216 | tf_op jit(solution)/shard_map/all_to_all | solution.py:87
  (26 shorter events, 7.3 us)
Async XLA Ops:
  7.2 85.9 %all-gather.5.cloned.1.call-start = ((), (), s32[]{:S(2)}) async-start(), calls=%async_computation.2 | async-start | bytes 3342336 | tf_op jit(solution)/shard_map/all_gather | solution.py:64
  34.1 124.3 %all-gather.3.cloned.1.call-start = ((), (), s32[]{:S(2)}) async-start(), calls=%async_computation.1 | async-start | bytes 6684672 | tf_op jit(solution)/shard_map/all_gather | solution.py:63
  95.1 82.9 %copy-start.1 = (bf16[768,32]{0,1:T(8,128)(2,1)S(1)}, bf16[768,32]{0,1:T(8,128)(2,1)}, u32[]{:S(2)}) copy-start(bf16[768,32]{0,1:T(8,128)(2,1)} %param.6) | copy-start | bytes 147460
  178.0 129.3 %copy-start = (f32[768,16]{0,1:T(8,128)S(1)}, f32[768,16]{0,1:T(8,128)}, u32[]{:S(2)}) copy-start(f32[768,16]{0,1:T(8,128)} %param.7) | copy-start | bytes 147460
  178.1 129.3 %copy-start.3 = (f32[16]{0:T(128)S(1)}, f32[16]{0:T(128)}, u32[]{:S(2)}) copy-start(f32[16]{0:T(128)} %param.8) | copy-start | bytes 196
  307.5 22.2 %copy-start.2 = (f32[768,16]{0,1:T(8,128)}, f32[768,16]{0,1:T(8,128)S(1)}, u32[]{:S(2)}) copy-start(f32[768,16]{0,1:T(8,128)S(1)} %multiply_add_fusion) | copy-start | bytes 147460
Sparse Core Ops, SparseCore 0:
  34.2 58.7 all-gather.4
  95.5 62.8 all-gather.2
where the time goes:
time: 338 us; the launch traced here: 336 us
  matrix products  96.4 us (29%)
  waiting for transfers between devices  94.5 us (28%)
  blocking collectives  67.3 us (20%)
  other arithmetic  36.5 us (11%)
  local copies, waits for them, and re-layouts  27.5 us (8%)
  between operations  14.1 us (4%)
    dot_general x12, matrix products, kernel_apply(): return jnp.dot(weights, coeffs, preferred_element_type=jnp.float32)  96.1 us
    all_gather x1, waiting for transfers between devices, body(): lax.all_gather(panel_x, 'blk', axis=0, tiled=True)  63.3 us
    reduce_sum x12, other arithmetic, kernel_apply(): col_norms = jnp.sum(wide_cols * wide_cols, axis=1)  33 us
    all_gather x1, waiting for transfers between devices, body(): lax.all_gather(panel_v, 'blk', axis=0, tiled=True)  31.2 us
    all_gather x1, blocking collectives, body(): lax.all_gather(half_dirs, 'rows', axis=0, tiled=True)  26.1 us
    all_gather x1, blocking collectives, body(): lax.all_gather(observation_points, 'rows', axis=0, tiled=True)  25.1 us
    all_gather x1, local copies, waits for them, and re-layouts, body(): lax.all_gather(panel_x, 'blk', axis=0, tiled=True)  19.6 us
    all_to_all x1, blocking collectives, body(): lax.all_to_all(buffer.reshape(devices, flat_len), ('blk', 'rows'), split_...  16.2 us
  transfers between devices with their start and end apart: 2, of which 2 were waited for; matrix products, arithmetic and copies ran while one was open for 1% of the time, Pallas kernels for 0%

commit v1 on v0

v1 whole, which is shorter than its diff:
```python
import functools

import jax
import jax.numpy as jnp
from jax import lax
from jax.experimental import pallas as pl
from jax.experimental.pallas import tpu as pltpu
from jax.sharding import PartitionSpec as P

FOLD_DEV = 4
SLOTS = 3
LANES = 128
WIDE = 256
FEAT = 32
RIDGE = 16
FPAD = 40
CHUNK = WIDE - FPAD
ROWS = 256
LOG2E = 1.4426950408889634


def thirds(value):
    high = value.astype(jnp.bfloat16).astype(jnp.float32)
    mid = (value - high).astype(jnp.bfloat16).astype(jnp.float32)
    low = (value - high - mid).astype(jnp.bfloat16).astype(jnp.float32)
    return high, mid, low


def widened(points, ones_first):
    parts = thirds(-0.5 * jnp.sum(points * points, axis=0, keepdims=True))
    row = lax.broadcasted_iota(jnp.int32, (FPAD - FEAT, points.shape[1]), 0)
    one_at, norm_at = (0, 3) if ones_first else (3, 0)
    extra = jnp.where((row >= one_at) & (row < one_at + 3), 1.0, 0.0)
    for step, part in enumerate(parts):
        extra = jnp.where(row == norm_at + step, part, extra)
    return jnp.concatenate([points, extra], axis=0)


def apply_body(*refs):
    rows = refs[3].shape[0] // 2
    step = ROWS if (rows // ROWS) % 2 == 0 else rows // 2
    pl.run_scoped(
        functools.partial(apply_scoped, step, *refs),
        *[pltpu.ACC(unit)((step, WIDE), jnp.float32) for unit in (0, 0, 1, 1)],
    )


def apply_scoped(step, xa_ref, xb_ref, out_ref, held, feats, total, columns, *sums):
    sums = (sums[:2], sums[2:])
    blocks_a, _, span = xa_ref.shape
    blocks_b = xb_ref.shape[0]
    groups = span // LANES
    rows_a, rows_b = blocks_a * span, blocks_b * span
    passes = -(-rows_b // CHUNK)
    half = rows_a // 2
    steps = half // step
    lane = lax.broadcasted_iota(jnp.int32, (1, LANES), 1)

    def fill_a(block, carry):
        for group in range(groups):
            points = xa_ref[block, :, group * LANES : (group + 1) * LANES].astype(jnp.float32)
            rest = jnp.zeros((LANES - FPAD, LANES), jnp.float32)
            turned = jnp.concatenate([widened(points, True), rest], axis=0).T.astype(jnp.bfloat16)
            at = pl.ds(pl.multiple_of(block * span + group * LANES, LANES), LANES)
            feats[at, :] = turned
            held[at, :LANES] = turned
        return carry

    lax.fori_loop(0, blocks_a, fill_a, 0)
    held[:, LANES:] = jnp.zeros((rows_a, LANES), jnp.bfloat16)
    total[...] = jnp.zeros_like(total)
    columns[:, :LANES] = jnp.zeros((columns.shape[0], LANES), jnp.float32)
    past = columns.shape[1] - LANES - rows_b
    columns[:, LANES + rows_b :] = jnp.zeros((columns.shape[0], past), jnp.float32)

    def fill_b(block, carry):
        at = pl.ds(pl.multiple_of(LANES + block * span, LANES), span)
        panel = xb_ref[block].astype(jnp.float32)
        columns[:FPAD, at] = widened(panel[:FEAT], False)
        columns[FPAD:, at] = panel[FEAT:]
        return carry

    lax.fori_loop(0, blocks_b, fill_b, 0)

    def window(number, low, high):
        start = LANES - FPAD + number * CHUNK
        base = pl.multiple_of((start // LANES) * LANES, LANES)
        shift = start % LANES
        parts = [
            pltpu.roll(columns[low:high, pl.ds(base + k * LANES, LANES)], (LANES - shift) % LANES, 1)
            for k in range(3)
        ]
        keep = lane < LANES - shift
        return jnp.where(keep, parts[0], parts[1]), jnp.where(keep, parts[1], parts[2])

    def stage(number):
        feat_0, feat_1 = window(jnp.minimum(number, passes), 0, FPAD)
        live = jnp.where(number < passes, 1.0, 0.0)
        feat_0 = jnp.where(lane < FPAD, 0.0, feat_0) * live
        dirs_0, dirs_1 = window(jnp.maximum(number - 1, 0), FPAD, FPAD + RIDGE)
        has = jnp.where(number > 0, 1.0, 0.0)
        rest = jnp.zeros((LANES - RIDGE, LANES), jnp.float32)
        turned_0 = jnp.concatenate([dirs_0 * has, rest], axis=0).T
        turned_1 = jnp.concatenate([dirs_1 * has, rest], axis=0).T
        left = jnp.concatenate([feat_0, turned_0[FPAD:], turned_1], axis=0)
        right = jnp.concatenate([feat_1 * live, jnp.zeros((CHUNK, LANES), jnp.float32)], axis=0)
        block = jnp.concatenate([left, right], axis=1).astype(jnp.bfloat16)
        pltpu.matmul_push_rhs(block, 0, 0)
        pltpu.matmul_push_rhs(block, 0, 1)

    keep_feats = lax.broadcasted_iota(jnp.int32, (step, LANES), 1) < FPAD

    def issue(unit, number, fresh):
        at = unit * half + number * step
        pltpu.matmul_acc_lhs(sums[unit][number % 2], held[at : at + step, :], load_staged_rhs=0 if fresh else None)

    def finish(unit, number, last):
        at = unit * half + number * step
        found = pltpu.matmul_pop(sums[unit][number % 2])
        total[at : at + step, :] += found[:, :LANES]
        if not last:
            weights = jnp.exp2(found * LOG2E).astype(jnp.bfloat16)
            held[at : at + step, :LANES] = jnp.where(keep_feats, feats[at : at + step, :], weights[:, :LANES])
            held[at : at + step, LANES:] = weights[:, LANES:]

    def one_pass(more, last):
        for number in range(steps):
            for unit in range(2):
                if number + 1 < steps:
                    issue(unit, number + 1, False)
                elif more:
                    issue(unit, 0, True)
                finish(unit, number, last)

    stage(0)
    for unit in range(2):
        issue(unit, 0, True)
    stage(1)

    def middle(number, carry):
        one_pass(True, False)
        stage(number + 2)
        return carry

    lax.fori_loop(0, passes - 1, middle, 0)
    one_pass(True, False)
    one_pass(False, True)
    for block in range(blocks_a):
        for group in range(groups):
            at = block * span + group * LANES
            out_ref[block, :, group * LANES : (group + 1) * LANES] = total[at : at + LANES, :].T[:RIDGE]


def apply_kernel(rows_of, columns_of):
    blocks_a, _, span = rows_of.shape
    rows_a, rows_b = blocks_a * span, columns_of.shape[0] * span
    passes = -(-rows_b // CHUNK)
    width = LANES + -(-(passes * CHUNK + 2 * WIDE) // LANES) * LANES
    return pl.pallas_call(
        apply_body,
        out_shape=jax.ShapeDtypeStruct((blocks_a, RIDGE, span), jnp.float32),
        scratch_shapes=[
            pltpu.VMEM((rows_a, WIDE), jnp.bfloat16),
            pltpu.VMEM((rows_a, LANES), jnp.bfloat16),
            pltpu.VMEM((rows_a, LANES), jnp.float32),
            pltpu.VMEM((FPAD + RIDGE, width), jnp.float32),
        ],
        compiler_params=pltpu.CompilerParams(vmem_limit_bytes=40 * 2**20),
        cost_estimate=pl.CostEstimate(
            flops=2 * rows_a * passes * WIDE * WIDE, bytes_accessed=3 * 2**20, transcendentals=rows_a * rows_b
        ),
        name="kernel_rows",
    )(rows_of, columns_of)


def scatter_body(devices, shares_ref, dirs_ref, ridge_ref, row_ids_ref, col_ids_ref, image_ref, send_ref):
    samples = dirs_ref.shape[1]
    dirs = dirs_ref[...]
    image = jnp.sum(shares_ref[...], axis=0) + ridge_ref[...] * dirs
    row_ids = row_ids_ref[...]
    rank = jnp.zeros((1, samples), jnp.int32)
    here = lax.broadcasted_iota(jnp.int32, (LANES, samples), 1)
    for group in range(samples // LANES):
        at = slice(group * LANES, (group + 1) * LANES)
        before = lax.broadcasted_iota(jnp.int32, (LANES, samples), 0) + group * LANES < here
        same = (col_ids_ref[at, :] == row_ids) & before
        rank += jnp.sum(jnp.where(same, 1, 0), axis=0, keepdims=True)
    owner = row_ids // FOLD_DEV
    place = (row_ids % FOLD_DEV) * SLOTS + rank
    pieces = thirds(jnp.concatenate([dirs, image], axis=0))
    rest = jnp.zeros((LANES - 6 * RIDGE, samples), jnp.float32)
    stacked = jnp.concatenate([*pieces, rest], axis=0)
    filler = jnp.zeros((LANES - RIDGE, LANES), jnp.float32)
    turned = []
    for group in range(samples // LANES):
        at = slice(group * LANES, (group + 1) * LANES)
        turned.append(stacked[:, at].T)
        image_ref[at, :] = jnp.concatenate([image[:, at], filler], axis=0).T[:, :RIDGE]
    turned = jnp.concatenate(turned, axis=0).astype(jnp.bfloat16)
    device = lax.broadcasted_iota(jnp.int32, (devices, samples), 0)
    for quad in range(FOLD_DEV * SLOTS // 4):
        found = []
        for slot in range(4 * quad, 4 * quad + 4):
            chosen = jnp.where((device == owner) & (place == slot), 1.0, 0.0).astype(jnp.bfloat16)
            parts = jnp.dot(chosen, turned, preferred_element_type=jnp.float32)
            found.append(parts[:, :32] + parts[:, 32:64] + parts[:, 64:96])
        send_ref[:, quad * LANES : (quad + 1) * LANES] = jnp.concatenate(found, axis=1)


def fold_body(scale, rows_ref, out_ref):
    rows = rows_ref[...]
    products = lax.dot_general(
        rows,
        rows,
        (((0,), (0,)), ((), ())),
        precision=lax.Precision.HIGHEST,
        preferred_element_type=jnp.float32,
    )
    for fold in range(FOLD_DEV):
        found = jnp.zeros((RIDGE, RIDGE), jnp.float32)
        for slot in range(fold * SLOTS, (fold + 1) * SLOTS):
            at = 2 * RIDGE * slot
            found += products[at : at + RIDGE, at + RIDGE : at + 2 * RIDGE]
        out_ref[fold] = found * scale


def body(observation_points, search_vectors, shrinkage_levels, holdout_group):
    samples = observation_points.shape[0]
    blk_count, row_count = lax.axis_size("blk"), lax.axis_size("rows")
    devices = blk_count * row_count
    points = observation_points.T
    dirs = search_vectors.T
    panel = jnp.concatenate([points, dirs.astype(jnp.bfloat16)], axis=0)
    rows_of = lax.all_to_all(jnp.broadcast_to(points, (row_count, *points.shape)), "rows", 0, 0, tiled=True)
    columns_of = lax.all_to_all(jnp.broadcast_to(panel, (blk_count, *panel.shape)), "blk", 0, 0, tiled=True)
    shares = lax.all_to_all(apply_kernel(rows_of, columns_of), "rows", 0, 0, tiled=True)
    image, send = pl.pallas_call(
        functools.partial(scatter_body, devices),
        out_shape=[
            jax.ShapeDtypeStruct((samples, RIDGE), jnp.float32),
            jax.ShapeDtypeStruct((devices, 2 * RIDGE * FOLD_DEV * SLOTS), jnp.float32),
        ],
        compiler_params=pltpu.CompilerParams(vmem_limit_bytes=40 * 2**20),
        name="image_and_slots",
    )(shares, dirs, shrinkage_levels[:, None], holdout_group.T, holdout_group)
    received = lax.all_to_all(send, ("blk", "rows"), 0, 0, tiled=True)
    folds = pl.pallas_call(
        functools.partial(fold_body, FOLD_DEV / samples),
        out_shape=jax.ShapeDtypeStruct((FOLD_DEV, RIDGE, RIDGE), jnp.float32),
        compiler_params=pltpu.CompilerParams(vmem_limit_bytes=40 * 2**20),
        name="fold_products",
    )(received)
    return image, folds.reshape(FOLD_DEV, RIDGE * RIDGE)


def solution(mesh):
    split = P(("blk", "rows"), None)
    return jax.shard_map(
        body,
        mesh=mesh,
        in_specs=(split, split, P(), split),
        out_specs=(split, split),
        check_vma=False,
    )
```

time: 338 us -> 142 us (0.42)
  matrix products: 96.4 us -> 0 us
  waiting for transfers between devices: 94.5 us -> 23.2 us
  Pallas kernels: 0 us -> 69.6 us
  blocking collectives: 67.3 us -> 27.9 us
  other arithmetic: 36.5 us -> 0.01 us
  local copies, waits for them, and re-layouts: 27.5 us -> 4.33 us
  starting transfers between devices: 0.08 us -> 16.2 us
  between operations: 14.1 us -> 0.73 us
    dot_general x13 -> x0, matrix products: 96.4 us -> none  [the longest x12 96.1 us: kernel_apply(): return jnp.dot(weights, coeffs, preferred_element_type=jnp.float32)]
    all_gather x2 -> x0, waiting for transfers between devices: 94.4 us -> none  [the longest x1 63.3 us: body(): lax.all_gather(panel_x, 'blk', axis=0, tiled=True)]
    pallas_call x0 -> x3, Pallas kernels: none -> 69.6 us  [the longest x1 67.5 us: apply_kernel(): pl.pallas_call(apply_body, out_shape=jax.ShapeDtypeStruct((blocks_a, RIDG...]
    all_gather x2 -> x0, blocking collectives: 51.1 us -> none  [the longest x1 26.1 us: body(): lax.all_gather(half_dirs, 'rows', axis=0, tiled=True)]
    reduce_sum x14 -> x0, other arithmetic: 34.2 us -> none  [the longest x12 33 us: kernel_apply(): col_norms = jnp.sum(wide_cols * wide_cols, axis=1)]
    all_to_all x0 -> x3, waiting for transfers between devices: none -> 23.2 us  [the longest x1 9.96 us: body(): received = lax.all_to_all(send, ('blk', 'rows'), 0, 0, tiled=True)]
    all_gather x1 -> x0, local copies, waits for them, and re-layouts: 19.6 us -> none  [body(): lax.all_gather(panel_x, 'blk', axis=0, tiled=True)]
    all_to_all x0 -> x3, starting transfers between devices: none -> 16.2 us  [the longest x1 6.79 us: body(): lax.all_to_all(jnp.broadcast_to(points, (row_count, *points.shape)), 'row...]
  transfers between devices with their start and end apart: 2 -> 3, of which waited for: 2 -> 3; matrix products, arithmetic and copies ran while one was open for 1% -> 1% of each run, Pallas kernels for 0% -> 0%
where the time goes in v1:
time: 142 us
  Pallas kernels  69.6 us (49%)
  blocking collectives  27.9 us (20%)
  waiting for transfers between devices  23.2 us (16%)
  starting transfers between devices  16.2 us (11%)
  local copies, waits for them, and re-layouts  4.33 us (3%)
    pallas_call x1, Pallas kernels, apply_kernel(): pl.pallas_call(apply_body, out_shape=jax.ShapeDtypeStruct((blocks_a, RIDG...  67.5 us
    all_to_all x1, blocking collectives, body(): lax.all_to_all(jnp.broadcast_to(panel, (blk_count, *panel.shape)), 'blk',...  27.9 us
    all_to_all x1, waiting for transfers between devices, body(): received = lax.all_to_all(send, ('blk', 'rows'), 0, 0, tiled=True)  9.96 us
    all_to_all x1, starting transfers between devices, body(): lax.all_to_all(jnp.broadcast_to(points, (row_count, *points.shape)), 'row...  6.79 us
    all_to_all x1, waiting for transfers between devices, body(): lax.all_to_all(jnp.broadcast_to(points, (row_count, *points.shape)), 'row...  6.76 us
    all_to_all x1, waiting for transfers between devices, body(): lax.all_to_all(apply_kernel(rows_of, columns_of), 'rows', 0, 0, tiled=True)  6.51 us
    all_to_all x1, starting transfers between devices, body(): received = lax.all_to_all(send, ('blk', 'rows'), 0, 0, tiled=True)  5.81 us
    all_to_all x1, starting transfers between devices, body(): lax.all_to_all(apply_kernel(rows_of, columns_of), 'rows', 0, 0, tiled=True)  3.58 us
  transfers between devices with their start and end apart: 3, of which 3 were waited for; matrix products, arithmetic and copies ran while one was open for 1% of the time, Pallas kernels for 0%

profile of v1, /device:TPU:1, one launch (start us, length us, event | category | flops | bytes accessed | tf_op | source)
XLA Modules:
  0.0 142.1 jit_solution(18181834480159613427)
XLA Ops:
  0.6 0.0 copy-start.2
  0.6 0.0 copy-start
  0.6 1.6 %broadcast_in_dim.9 = bf16[8,32,768]{2,1,0:T(8,128)(2,1)} broadcast(bf16[32,768]{1,0:T(8,128)(2,1)} %bitcast.13), dimensions={1,2} | broadcast | bytes 442368 | tf_op jit(solution)/shard_map/broadcast_in_dim | solution.py:234
  2.3 6.8 %all-to-all-start = ((bf16[8,32,768]{2,1,0:T(8,128)(2,1)}), bf16[8,32,768]{2,1,0:T(8,128)(2,1)S(1)}, u32[]{:S(2)}, u32[]{:S(2)}) async-start(bf16[8,32,768]{2,1,0:T(8,128)(2,1)} %broadcast_in_dim.9), calls=%async_computation | async-start | bytes 786432 | tf_op jit(solution)/shard_map/all_to_all | solution.py:234
  9.1 0.0 copy-done
  9.1 0.0 copy-done.2
  9.1 6.8 %all-to-all-done.refs_0_ = bf16[8,32,768]{2,1,0:T(8,128)(2,1)S(1)} async-done(((bf16[8,32,768]{2,1,0:T(8,128)(2,1)}), bf16[8,32,768]{2,1,0:T(8,128)(2,1)S(1)}, u32[]{:S(2)}, u32[]{:S(2)}) %all-to-all-start) | async-done | bytes 393248 | tf_op jit(solution)/shard_map/all_to_all | solution.py:234
  15.9 0.1 broadcast_in_dim.10
  16.0 27.9 %all_to_all.26.refs_1_ = bf16[16,48,768]{2,1,0:T(8,128)(2,1)S(1)} all-to-all(bf16[16,48,768]{2,1,0:T(8,128)(2,1)S(1)} %broadcast_in_dim.10), channel_id=1, replica_groups=mesh['blk'=16,'rows'=8] {'blk'}, dimensions={0} | all-to-all | bytes 2359296 | tf_op jit(solution)/shard_map/all_to_all | solution.py:235
  43.9 0.0 copy-start.1
  43.9 67.5 %kernel_rows.1 = f32[8,16,768]{2,1,0:T(8,128)} custom-call(bf16[8,32,768]{2,1,0:T(8,128)(2,1)S(1)} %all-to-all-done.refs_0_, bf16[16,48,768]{2,1,0:T(8,128)(2,1)S(1)} %all_to_all.26.refs_1_), custom_call_target="tpu_custom_call" | custom-call | flops 45902462976 | bytes 3145728 | tf_op jit(solution)/shard_map/kernel_rows/pallas_call | solution.py:159
  111.4 0.0 copy-start.3
  111.4 3.6 %all-to-all-start.2 = ((f32[8,16,768]{2,1,0:T(8,128)}), f32[8,16,768]{2,1,0:T(8,128)S(1)}, u32[]{:S(2)}, u32[]{:S(2)}) async-start(f32[8,16,768]{2,1,0:T(8,128)} %kernel_rows.1), calls=%async_computation.2 | async-start | bytes 786432 | tf_op jit(solution)/shard_map/all_to_all | solution.py:236
  115.0 0.0 copy-done.1
  115.0 0.2 copy.10.col_ids_ref
  115.2 0.0 copy-done.3
  115.2 0.1 copy.9.ridge_ref
  115.3 6.5 %all-to-all-done.2.shares_ref = f32[8,16,768]{2,1,0:T(8,128)S(1)} async-done(((f32[8,16,768]{2,1,0:T(8,128)}), f32[8,16,768]{2,1,0:T(8,128)S(1)}, u32[]{:S(2)}, u32[]{:S(2)}) %all-to-all-start.2) | async-done | bytes 393248 | tf_op jit(solution)/shard_map/all_to_all | solution.py:236
  121.8 1.3 image_and_slots.1
  123.1 0.9 copy.11
  124.0 5.8 %all-to-all-start.3 = ((f32[128,1,384]{2,1,0:T(1,128)}), f32[128,1,384]{2,1,0:T(1,128)S(1)}, u32[]{:S(2)}, u32[]{:S(2)}) async-start(f32[128,1,384]{2,1,0:T(1,128)} %copy.11), calls=%async_computation.3 | async-start | bytes 393216 | tf_op jit(solution)/shard_map/all_to_all | solution.py:246
  129.8 0.8 copy.12
  130.6 10.0 %all-to-all-done.3 = f32[128,1,384]{2,1,0:T(1,128)S(1)} async-done(((f32[128,1,384]{2,1,0:T(1,128)}), f32[128,1,384]{2,1,0:T(1,128)S(1)}, u32[]{:S(2)}, u32[]{:S(2)}) %all-to-all-start.3) | async-done | bytes 196640 | tf_op jit(solution)/shard_map/all_to_all | solution.py:246
  140.6 0.8 fold_products.1
  141.4 0.7 reshape.9
  (3 shorter events, 0.0 us)
Async XLA Ops:
  0.6 8.5 %copy-start.2 = (bf16[768,32]{0,1:T(8,128)(2,1)S(1)}, bf16[768,32]{0,1:T(8,128)(2,1)}, u32[]{:S(2)}) copy-start(bf16[768,32]{0,1:T(8,128)(2,1)} %param.4) | copy-start | bytes 147460
  0.6 8.4 %copy-start = (f32[768,16]{0,1:T(8,128)S(1)}, f32[768,16]{0,1:T(8,128)}, u32[]{:S(2)}) copy-start(f32[768,16]{0,1:T(8,128)} %param.5) | copy-start | bytes 147460
  2.3 13.6 %all-to-all-start = ((bf16[8,32,768]{2,1,0:T(8,128)(2,1)}), bf16[8,32,768]{2,1,0:T(8,128)(2,1)S(1)}, u32[]{:S(2)}, u32[]{:S(2)}) async-start(bf16[8,32,768]{2,1,0:T(8,128)(2,1)} %broadcast_in_dim.9), calls=%async_computation | async-start | bytes 786432 | tf_op jit(solution)/shard_map/all_to_all | solution.py:234
  43.9 71.1 %copy-start.1 = (s32[768,1]{0,1:T(1,128)S(1)}, s32[768,1]{0,1:T(1,128)}, u32[]{:S(2)}) copy-start(s32[768,1]{0,1:T(1,128)} %param.7) | copy-start | bytes 9220
  111.4 3.8 %copy-start.3 = (f32[16]{0:T(128)S(1)}, f32[16]{0:T(128)}, u32[]{:S(2)}) copy-start(f32[16]{0:T(128)} %param.6) | copy-start | bytes 196
  111.4 10.4 %all-to-all-start.2 = ((f32[8,16,768]{2,1,0:T(8,128)}), f32[8,16,768]{2,1,0:T(8,128)S(1)}, u32[]{:S(2)}, u32[]{:S(2)}) async-start(f32[8,16,768]{2,1,0:T(8,128)} %kernel_rows.1), calls=%async_computation.2 | async-start | bytes 786432 | tf_op jit(solution)/shard_map/all_to_all | solution.py:236
  124.0 16.5 %all-to-all-start.3 = ((f32[128,1,384]{2,1,0:T(1,128)}), f32[128,1,384]{2,1,0:T(1,128)S(1)}, u32[]{:S(2)}, u32[]{:S(2)}) async-start(f32[128,1,384]{2,1,0:T(1,128)} %copy.11), calls=%async_computation.3 | async-start | bytes 393216 | tf_op jit(solution)/shard_map/all_to_all | solution.py:246

commit v2 on v1

--- a/solution.py
+++ b/solution.py
@@ -15,7 +15,7 @@
 RIDGE = 16
 FPAD = 40
 CHUNK = WIDE - FPAD
-ROWS = 256
+STEPS = 8
 LOG2E = 1.4426950408889634
 
 
@@ -37,20 +37,19 @@
 
 
 def apply_body(*refs):
-    rows = refs[3].shape[0] // 2
-    step = ROWS if (rows // ROWS) % 2 == 0 else rows // 2
+    step = refs[4].shape[0] // (2 * STEPS)
     pl.run_scoped(
         functools.partial(apply_scoped, step, *refs),
         *[pltpu.ACC(unit)((step, WIDE), jnp.float32) for unit in (0, 0, 1, 1)],
     )
 
 
-def apply_scoped(step, xa_ref, xb_ref, out_ref, held, feats, total, columns, *sums):
+def apply_scoped(step, xa_ref, xb_ref, xc_ref, out_ref, held, feats, total, columns, scale, *sums):
     sums = (sums[:2], sums[2:])
     blocks_a, _, span = xa_ref.shape
     blocks_b = xb_ref.shape[0]
     groups = span // LANES
-    rows_a, rows_b = blocks_a * span, blocks_b * span
+    rows_a, rows_b = blocks_a * span, 2 * blocks_b * span
     passes = -(-rows_b // CHUNK)
     half = rows_a // 2
     steps = half // step
@@ -74,10 +73,11 @@
     columns[:, LANES + rows_b :] = jnp.zeros((columns.shape[0], past), jnp.float32)
 
     def fill_b(block, carry):
-        at = pl.ds(pl.multiple_of(LANES + block * span, LANES), span)
-        panel = xb_ref[block].astype(jnp.float32)
-        columns[:FPAD, at] = widened(panel[:FEAT], False)
-        columns[FPAD:, at] = panel[FEAT:]
+        for place, ref in ((block, xb_ref), (blocks_b + block, xc_ref)):
+            at = pl.ds(pl.multiple_of(LANES + place * span, LANES), span)
+            panel = ref[block].astype(jnp.float32)
+            columns[:FPAD, at] = widened(panel[:FEAT], False)
+            columns[FPAD:, at] = panel[FEAT:]
         return carry
 
     lax.fori_loop(0, blocks_b, fill_b, 0)
@@ -108,6 +108,8 @@
         pltpu.matmul_push_rhs(block, 0, 0)
         pltpu.matmul_push_rhs(block, 0, 1)
 
+    scale[...] = jnp.full(scale.shape, LOG2E, jnp.float32)
+    to_base_2 = scale[0:1, :]
     keep_feats = lax.broadcasted_iota(jnp.int32, (step, LANES), 1) < FPAD
 
     def issue(unit, number, fresh):
@@ -119,7 +121,7 @@
         found = pltpu.matmul_pop(sums[unit][number % 2])
         total[at : at + step, :] += found[:, :LANES]
         if not last:
-            weights = jnp.exp2(found * LOG2E).astype(jnp.bfloat16)
+            weights = jnp.exp2(found * to_base_2).astype(jnp.bfloat16)
             held[at : at + step, :LANES] = jnp.where(keep_feats, feats[at : at + step, :], weights[:, :LANES])
             held[at : at + step, LANES:] = weights[:, LANES:]
 
@@ -151,9 +153,9 @@
             out_ref[block, :, group * LANES : (group + 1) * LANES] = total[at : at + LANES, :].T[:RIDGE]
 
 
-def apply_kernel(rows_of, columns_of):
+def apply_kernel(rows_of, columns_of, more_columns):
     blocks_a, _, span = rows_of.shape
-    rows_a, rows_b = blocks_a * span, columns_of.shape[0] * span
+    rows_a, rows_b = blocks_a * span, 2 * columns_of.shape[0] * span
     passes = -(-rows_b // CHUNK)
     width = LANES + -(-(passes * CHUNK + 2 * WIDE) // LANES) * LANES
     return pl.pallas_call(
@@ -164,19 +166,21 @@
             pltpu.VMEM((rows_a, LANES), jnp.bfloat16),
             pltpu.VMEM((rows_a, LANES), jnp.float32),
             pltpu.VMEM((FPAD + RIDGE, width), jnp.float32),
+            pltpu.VMEM((8, WIDE), jnp.float32),
         ],
         compiler_params=pltpu.CompilerParams(vmem_limit_bytes=40 * 2**20),
         cost_estimate=pl.CostEstimate(
             flops=2 * rows_a * passes * WIDE * WIDE, bytes_accessed=3 * 2**20, transcendentals=rows_a * rows_b
         ),
         name="kernel_rows",
-    )(rows_of, columns_of)
+    )(rows_of, columns_of, more_columns)
 
 
 def scatter_body(devices, shares_ref, dirs_ref, ridge_ref, row_ids_ref, col_ids_ref, image_ref, send_ref):
     samples = dirs_ref.shape[1]
     dirs = dirs_ref[...]
     image = jnp.sum(shares_ref[...], axis=0) + ridge_ref[...] * dirs
+    image_ref[...] = image
     row_ids = row_ids_ref[...]
     rank = jnp.zeros((1, samples), jnp.int32)
     here = lax.broadcasted_iota(jnp.int32, (LANES, samples), 1)
@@ -190,12 +194,7 @@
     pieces = thirds(jnp.concatenate([dirs, image], axis=0))
     rest = jnp.zeros((LANES - 6 * RIDGE, samples), jnp.float32)
     stacked = jnp.concatenate([*pieces, rest], axis=0)
-    filler = jnp.zeros((LANES - RIDGE, LANES), jnp.float32)
-    turned = []
-    for group in range(samples // LANES):
-        at = slice(group * LANES, (group + 1) * LANES)
-        turned.append(stacked[:, at].T)
-        image_ref[at, :] = jnp.concatenate([image[:, at], filler], axis=0).T[:, :RIDGE]
+    turned = [stacked[:, group * LANES : (group + 1) * LANES].T for group in range(samples // LANES)]
     turned = jnp.concatenate(turned, axis=0).astype(jnp.bfloat16)
     device = lax.broadcasted_iota(jnp.int32, (devices, samples), 0)
     for quad in range(FOLD_DEV * SLOTS // 4):
@@ -204,11 +203,11 @@
             chosen = jnp.where((device == owner) & (place == slot), 1.0, 0.0).astype(jnp.bfloat16)
             parts = jnp.dot(chosen, turned, preferred_element_type=jnp.float32)
             found.append(parts[:, :32] + parts[:, 32:64] + parts[:, 64:96])
-        send_ref[:, quad * LANES : (quad + 1) * LANES] = jnp.concatenate(found, axis=1)
+        send_ref[:, 0, quad * LANES : (quad + 1) * LANES] = jnp.concatenate(found, axis=1)
 
 
 def fold_body(scale, rows_ref, out_ref):
-    rows = rows_ref[...]
+    rows = rows_ref[:, 0, :]
     products = lax.dot_general(
         rows,
         rows,
@@ -221,7 +220,8 @@
         for slot in range(fold * SLOTS, (fold + 1) * SLOTS):
             at = 2 * RIDGE * slot
             found += products[at : at + RIDGE, at + RIDGE : at + 2 * RIDGE]
-        out_ref[fold] = found * scale
+        lines = [found[line : line + 1, :] for line in range(RIDGE)]
+        out_ref[fold : fold + 1, :] = jnp.concatenate(lines, axis=1) * scale
 
 
 def body(observation_points, search_vectors, shrinkage_levels, holdout_group):
@@ -232,13 +232,22 @@
     dirs = search_vectors.T
     panel = jnp.concatenate([points, dirs.astype(jnp.bfloat16)], axis=0)
     rows_of = lax.all_to_all(jnp.broadcast_to(points, (row_count, *points.shape)), "rows", 0, 0, tiled=True)
-    columns_of = lax.all_to_all(jnp.broadcast_to(panel, (blk_count, *panel.shape)), "blk", 0, 0, tiled=True)
-    shares = lax.all_to_all(apply_kernel(rows_of, columns_of), "rows", 0, 0, tiled=True)
+    pairs = blk_count // 2
+    columns_of = lax.all_to_all(
+        jnp.broadcast_to(panel, (pairs, *panel.shape)),
+        "blk",
+        0,
+        0,
+        tiled=True,
+        axis_index_groups=[[2 * pair + core for pair in range(pairs)] for core in range(2)],
+    )
+    more_columns = lax.ppermute(columns_of, "blk", [(place, place ^ 1) for place in range(blk_count)])
+    shares = lax.all_to_all(apply_kernel(rows_of, columns_of, more_columns), "rows", 0, 0, tiled=True)
     image, send = pl.pallas_call(
         functools.partial(scatter_body, devices),
         out_shape=[
-            jax.ShapeDtypeStruct((samples, RIDGE), jnp.float32),
-            jax.ShapeDtypeStruct((devices, 2 * RIDGE * FOLD_DEV * SLOTS), jnp.float32),
+            jax.ShapeDtypeStruct((RIDGE, samples), jnp.float32),
+            jax.ShapeDtypeStruct((devices, 1, 2 * RIDGE * FOLD_DEV * SLOTS), jnp.float32),
         ],
         compiler_params=pltpu.CompilerParams(vmem_limit_bytes=40 * 2**20),
         name="image_and_slots",
@@ -246,11 +255,11 @@
     received = lax.all_to_all(send, ("blk", "rows"), 0, 0, tiled=True)
     folds = pl.pallas_call(
         functools.partial(fold_body, FOLD_DEV / samples),
-        out_shape=jax.ShapeDtypeStruct((FOLD_DEV, RIDGE, RIDGE), jnp.float32),
+        out_shape=jax.ShapeDtypeStruct((FOLD_DEV, RIDGE * RIDGE), jnp.float32),
         compiler_params=pltpu.CompilerParams(vmem_limit_bytes=40 * 2**20),
         name="fold_products",
     )(received)
-    return image, folds.reshape(FOLD_DEV, RIDGE * RIDGE)
+    return image.T, folds
 
 
 def solution(mesh):

time: 142 us -> 121 us (0.85)
  blocking collectives: 27.9 us -> 47.7 us
  waiting for transfers between devices: 23.2 us -> 5.12 us
  Pallas kernels: 69.6 us -> 59.1 us
  starting transfers between devices: 16.2 us -> 6.01 us
  local copies, waits for them, and re-layouts: 4.33 us -> 1.59 us
    all_to_all x1 -> x3, blocking collectives: 27.9 us -> 47.7 us  [the longest x1 18.4 us: body(): lax.all_to_all(jnp.broadcast_to(panel, (pairs, *panel.shape)), 'blk', 0,...]
    all_to_all x3 -> x1, waiting for transfers between devices: 23.2 us -> 5.12 us  [body(): lax.all_to_all(apply_kernel(rows_of, columns_of, more_columns), 'rows', 0...]
    all_to_all x3 -> x1, starting transfers between devices: 16.2 us -> 3.73 us  [body(): lax.all_to_all(apply_kernel(rows_of, columns_of, more_columns), 'rows', 0...]
    pallas_call x1, Pallas kernels: 67.5 us -> 55.8 us  [apply_kernel(): pl.pallas_call(apply_body, out_shape=jax.ShapeDtypeStruct((blocks_a, RIDG...]
    ppermute x0 -> x1, starting transfers between devices: none -> 2.28 us  [body(): lax.ppermute(columns_of, 'blk', [(place, place ^ 1) for place in range(bl...]
    broadcast_in_dim x1, local copies, waits for them, and re-layouts: 1.63 us -> 0.03 us  [body(): jnp.broadcast_to(points, (row_count, *points.shape))]
  transfers between devices with their start and end apart: 3 -> 2, of which waited for: 3 -> 1; matrix products, arithmetic and copies ran while one was open for 1% -> 0% of each run, Pallas kernels for 0% -> 0%
where the time goes in v2:
time: 121 us
  Pallas kernels  59.1 us (49%)
  blocking collectives  47.7 us (39%)
  starting transfers between devices  6.01 us (5%)
  waiting for transfers between devices  5.12 us (4%)
  local copies, waits for them, and re-layouts  1.59 us (1%)
    pallas_call x1, Pallas kernels, apply_kernel(): pl.pallas_call(apply_body, out_shape=jax.ShapeDtypeStruct((blocks_a, RIDG...  55.8 us
    all_to_all x1, blocking collectives, body(): lax.all_to_all(jnp.broadcast_to(panel, (pairs, *panel.shape)), 'blk', 0,...  18.4 us
    all_to_all x1, blocking collectives, body(): received = lax.all_to_all(send, ('blk', 'rows'), 0, 0, tiled=True)  16.6 us
    all_to_all x1, blocking collectives, body(): lax.all_to_all(jnp.broadcast_to(points, (row_count, *points.shape)), 'row...  12.7 us
    all_to_all x1, waiting for transfers between devices, body(): lax.all_to_all(apply_kernel(rows_of, columns_of, more_columns), 'rows', 0...  5.12 us
    all_to_all x1, starting transfers between devices, body(): lax.all_to_all(apply_kernel(rows_of, columns_of, more_columns), 'rows', 0...  3.73 us
  transfers between devices with their start and end apart: 2, of which 1 were waited for; matrix products, arithmetic and copies ran while one was open for 0% of the time, Pallas kernels for 0%

profile of v2, /device:TPU:1, one launch (start us, length us, event | category | flops | bytes accessed | tf_op | source)
XLA Modules:
  0.0 121.0 jit_solution(12413774302469409258)
XLA Ops:
  0.6 0.0 copy-start.2
  0.6 0.8 bitcast_convert_fusion
  1.5 0.0 copy-done.2
  1.5 18.4 %all_to_all.20.refs_1_ = bf16[8,48,768]{2,1,0:T(8,128)(2,1)S(1)} all-to-all(bf16[8,48,768]{2,1,0:T(8,128)(2,1)S(1)} %broadcast_in_dim.10), channel_id=1, replica_groups={{0,16,32,48,64,80,96,112},{8,24,40,56,72,88,104,120},{1,17,33,49,65,81,..., dimensions={0} | all-to-all | bytes 1179648 | tf_op jit(solution)/shard_map/all_to_all | solution.py:236
  19.9 2.3 %collective-permute-start = (bf16[8,48,768]{2,1,0:T(8,128)(2,1)S(1)}, bf16[8,48,768]{2,1,0:T(8,128)(2,1)S(1)}, u32[]{:S(2)}, u32[]{:S(2)}) collective-permute-start(bf16[8,48,768]{2,1,0:T(8,128)(2,1)S(1)} %all_to_all.20.refs_1_), channel_id=1, source_target_pairs={{0,8},{8,0},{16,24},{24,16},{32,40},{40,32},{48,56},{56,48},{64,72... | collective-permute-start | bytes 1769480 | tf_op jit(solution)/shard_map/ppermute | solution.py:244
  22.2 12.7 %all_to_all.21.refs_0_ = bf16[8,32,768]{2,1,0:T(8,128)(2,1)S(1)} all-to-all(bf16[8,32,768]{2,1,0:T(8,128)(2,1)S(1)} %broadcast_in_dim.9), channel_id=1, replica_groups=mesh['blk'=16,'rows'=8] {'rows'}, dimensions={0} | all-to-all | bytes 786432 | tf_op jit(solution)/shard_map/all_to_all | solution.py:234
  34.9 0.0 collective-permute-done.refs_2_
  34.9 55.8 %kernel_rows.1 = f32[8,16,768]{2,1,0:T(8,128)} custom-call(bf16[8,32,768]{2,1,0:T(8,128)(2,1)S(1)} %all_to_all.21.refs_0_, bf16[8,48,768]{2,1,0:T(8,128)(2,1)S(1)} %all_to_all.20.refs_1_, bf16[8,48,768]{2,1,0:T(8,128)(2,1)S(1)} %collective-permute-done.refs_2_), custom_call_target="tpu_custom_call" | custom-call | flops 45902462976 | bytes 3145728 | tf_op jit(solution)/shard_map/kernel_rows/pallas_call | solution.py:161
  90.7 3.7 %all-to-all-start.2 = ((f32[8,16,768]{2,1,0:T(8,128)}), f32[8,16,768]{2,1,0:T(8,128)S(1)}, u32[]{:S(2)}, u32[]{:S(2)}) async-start(f32[8,16,768]{2,1,0:T(8,128)} %kernel_rows.1), calls=%async_computation.2 | async-start | bytes 786432 | tf_op jit(solution)/shard_map/all_to_all | solution.py:245
  94.4 0.0 copy-start.3
  94.4 0.7 copy-done.3
  95.1 0.0 copy-start.1
  95.1 0.1 copy.6.ridge_ref
  95.2 0.6 copy-done.1
  95.8 0.0 copy-start
  95.8 0.2 copy.7.col_ids_ref
  95.9 5.1 %all-to-all-done.2.shares_ref = f32[8,16,768]{2,1,0:T(8,128)S(1)} async-done(((f32[8,16,768]{2,1,0:T(8,128)}), f32[8,16,768]{2,1,0:T(8,128)S(1)}, u32[]{:S(2)}, u32[]{:S(2)}) %all-to-all-start.2) | async-done | bytes 393248 | tf_op jit(solution)/shard_map/all_to_all | solution.py:245
  101.1 0.0 copy-done
  101.1 1.9 %image_and_slots.1 = (f32[16,768]{1,0:T(8,128)}, f32[128,1,384]{2,1,0:T(1,128)S(1)}) custom-call(f32[8,16,768]{2,1,0:T(8,128)S(1)} %all-to-all-done.2.shares_ref, f32[16,768]{1,0:T(8,128)S(1)} %bitcast.6, f32[16,1]{1,0:T(8,128)S(1)} %copy.6.ridge_ref, s32[1,768]{1,0:T(1,128)S(1)} %bitcast.7, s32[768,1]{1,0:T(8,128)S(1)} %copy.7.col_ids_ref), custom_call_target="tpu_custom_call" | custom-call | tf_op jit(solution)/shard_map/image_and_slots/pallas_call | solution.py:246
  102.9 16.6 %all_to_all.22.rows_ref = f32[128,1,384]{2,1,0:T(1,128)S(1)} all-to-all(f32[128,1,384]{2,1,0:T(1,128)S(1)} %get-tuple-element.5), channel_id=1, replica_groups=mesh['blk'=16,'rows'=8] {'blk','rows'}, dimensions={0} | all-to-all | bytes 393216 | tf_op jit(solution)/shard_map/all_to_all | solution.py:255
  119.5 1.4 %fold_products.1 = f32[4,256]{1,0:T(4,128)} custom-call(f32[128,1,384]{2,1,0:T(1,128)S(1)} %all_to_all.22.rows_ref), custom_call_target="tpu_custom_call" | custom-call | tf_op jit(solution)/shard_map/fold_products/pallas_call | solution.py:256
  (3 shorter events, 0.1 us)
Async XLA Ops:
  0.6 0.8 copy-start.2
  19.9 15.1 %collective-permute-start = (bf16[8,48,768]{2,1,0:T(8,128)(2,1)S(1)}, bf16[8,48,768]{2,1,0:T(8,128)(2,1)S(1)}, u32[]{:S(2)}, u32[]{:S(2)}) collective-permute-start(bf16[8,48,768]{2,1,0:T(8,128)(2,1)S(1)} %all_to_all.20.refs_1_), channel_id=1, source_target_pairs={{0,8},{8,0},{16,24},{24,16},{32,40},{40,32},{48,56},{56,48},{64,72... | collective-permute-start | bytes 1769480 | tf_op jit(solution)/shard_map/ppermute | solution.py:244
  90.7 10.4 %all-to-all-start.2 = ((f32[8,16,768]{2,1,0:T(8,128)}), f32[8,16,768]{2,1,0:T(8,128)S(1)}, u32[]{:S(2)}, u32[]{:S(2)}) async-start(f32[8,16,768]{2,1,0:T(8,128)} %kernel_rows.1), calls=%async_computation.2 | async-start | bytes 786432 | tf_op jit(solution)/shard_map/all_to_all | solution.py:245
  94.4 0.7 copy-start.3
  95.1 0.7 copy-start.1
  95.8 5.3 %copy-start = (f32[768,16]{0,1:T(8,128)S(1)}, f32[768,16]{0,1:T(8,128)}, u32[]{:S(2)}) copy-start(f32[768,16]{0,1:T(8,128)} %param.5) | copy-start | bytes 147460

commit v3 on v2

--- a/solution.py
+++ b/solution.py
@@ -9,6 +9,7 @@
 
 FOLD_DEV = 4
 SLOTS = 3
+SPOTS = 1024
 LANES = 128
 WIDE = 256
 FEAT = 32
@@ -16,6 +17,7 @@
 FPAD = 40
 CHUNK = WIDE - FPAD
 STEPS = 8
+TURNS = 2
 LOG2E = 1.4426950408889634
 
 
@@ -36,21 +38,24 @@
     return jnp.concatenate([points, extra], axis=0)
 
 
-def apply_body(*refs):
-    step = refs[4].shape[0] // (2 * STEPS)
+def apply_body(skip, *refs):
+    step = refs[-5].shape[0] // (2 * STEPS)
     pl.run_scoped(
-        functools.partial(apply_scoped, step, *refs),
+        functools.partial(apply_scoped, skip, step, *refs),
         *[pltpu.ACC(unit)((step, WIDE), jnp.float32) for unit in (0, 0, 1, 1)],
     )
 
 
-def apply_scoped(step, xa_ref, xb_ref, xc_ref, out_ref, held, feats, total, columns, scale, *sums):
+def apply_scoped(skip, step, *refs):
+    if skip:
+        own_ref, before_ref, near_ref, *refs = refs
+    xa_ref, xb_ref, xc_ref, out_ref, held, feats, total, columns, scale, *sums = refs
     sums = (sums[:2], sums[2:])
     blocks_a, _, span = xa_ref.shape
-    blocks_b = xb_ref.shape[0]
+    blocks_b = xb_ref.shape[0] - skip
     groups = span // LANES
     rows_a, rows_b = blocks_a * span, 2 * blocks_b * span
-    passes = -(-rows_b // CHUNK)
+    passes = passes_of(span, blocks_b, skip)
     half = rows_a // 2
     steps = half // step
     lane = lax.broadcasted_iota(jnp.int32, (1, LANES), 1)
@@ -75,12 +80,19 @@
     def fill_b(block, carry):
         for place, ref in ((block, xb_ref), (blocks_b + block, xc_ref)):
             at = pl.ds(pl.multiple_of(LANES + place * span, LANES), span)
-            panel = ref[block].astype(jnp.float32)
+            source = lax.rem(own_ref[0] + 1 + block, blocks_b + 1) if skip else block
+            panel = ref[source].astype(jnp.float32)
             columns[:FPAD, at] = widened(panel[:FEAT], False)
             columns[FPAD:, at] = panel[FEAT:]
         return carry
 
     lax.fori_loop(0, blocks_b, fill_b, 0)
+    if skip:
+        left = 2 * span % CHUNK
+        panel = near_ref[:, span - LANES :].astype(jnp.float32)
+        panel = jnp.concatenate([widened(panel[:FEAT], False), panel[FEAT:]], axis=0)
+        at = slice(LANES + rows_b, 2 * LANES + rows_b)
+        columns[:, at] = jnp.where(lane < left, pltpu.roll(panel, left, 1), 0.0)
 
     def window(number, low, high):
         start = LANES - FPAD + number * CHUNK
@@ -139,28 +151,45 @@
         issue(unit, 0, True)
     stage(1)
 
-    def middle(number, carry):
+    def middle(trip, carry):
+        for turn in range(TURNS):
+            one_pass(True, False)
+            stage(trip * TURNS + turn + 2)
+        return carry
+
+    trips = (passes - 1) // TURNS
+    lax.fori_loop(0, trips, middle, 0)
+    for number in range(trips * TURNS, passes - 1):
         one_pass(True, False)
         stage(number + 2)
-        return carry
-
-    lax.fori_loop(0, passes - 1, middle, 0)
     one_pass(True, False)
     one_pass(False, True)
     for block in range(blocks_a):
         for group in range(groups):
             at = block * span + group * LANES
-            out_ref[block, :, group * LANES : (group + 1) * LANES] = total[at : at + LANES, :].T[:RIDGE]
-
-
-def apply_kernel(rows_of, columns_of, more_columns):
+            lanes = slice(group * LANES, (group + 1) * LANES)
+            found = total[at : at + LANES, :].T[:RIDGE]
+            out_ref[block, :, lanes] = found + before_ref[block, :, lanes] if skip else found
+
+
+def passes_of(span, blocks_b, skip):
+    if not skip:
+        return 2 * blocks_b * span // CHUNK
+    return -(-(2 * blocks_b * span + 2 * span % CHUNK) // CHUNK)
+
+
+def apply_kernel(rows_of, columns_of, more_columns, own=None, before=None, near=None):
+    skip = own is not None
     blocks_a, _, span = rows_of.shape
-    rows_a, rows_b = blocks_a * span, 2 * columns_of.shape[0] * span
-    passes = -(-rows_b // CHUNK)
+    blocks_b = columns_of.shape[0] - skip
+    rows_a, rows_b = blocks_a * span, 2 * blocks_b * span
+    passes = passes_of(span, blocks_b, skip)
     width = LANES + -(-(passes * CHUNK + 2 * WIDE) // LANES) * LANES
+    whole = pl.BlockSpec(memory_space=pltpu.VMEM)
     return pl.pallas_call(
-        apply_body,
+        functools.partial(apply_body, skip),
         out_shape=jax.ShapeDtypeStruct((blocks_a, RIDGE, span), jnp.float32),
+        in_specs=[pl.BlockSpec(memory_space=pltpu.SMEM), whole, whole] * skip + [whole] * 3,
         scratch_shapes=[
             pltpu.VMEM((rows_a, WIDE), jnp.bfloat16),
             pltpu.VMEM((rows_a, LANES), jnp.bfloat16),
@@ -172,35 +201,44 @@
         cost_estimate=pl.CostEstimate(
             flops=2 * rows_a * passes * WIDE * WIDE, bytes_accessed=3 * 2**20, transcendentals=rows_a * rows_b
         ),
-        name="kernel_rows",
-    )(rows_of, columns_of, more_columns)
-
-
-def scatter_body(devices, shares_ref, dirs_ref, ridge_ref, row_ids_ref, col_ids_ref, image_ref, send_ref):
-    samples = dirs_ref.shape[1]
-    dirs = dirs_ref[...]
-    image = jnp.sum(shares_ref[...], axis=0) + ridge_ref[...] * dirs
-    image_ref[...] = image
-    row_ids = row_ids_ref[...]
+        name="kernel_rows_rest" if skip else "kernel_rows",
+    )(*([own, before, near] if skip else []), rows_of, columns_of, more_columns)
+
+
+def place_body(ids_ref, dirs_ref, place_ref, copy_ref):
+    ids = ids_ref[...]
+    samples = ids.shape[1]
+    named = ids.astype(jnp.float32)
     rank = jnp.zeros((1, samples), jnp.int32)
     here = lax.broadcasted_iota(jnp.int32, (LANES, samples), 1)
     for group in range(samples // LANES):
         at = slice(group * LANES, (group + 1) * LANES)
+        turned = jnp.broadcast_to(named[:, at], (LANES, LANES)).T
         before = lax.broadcasted_iota(jnp.int32, (LANES, samples), 0) + group * LANES < here
-        same = (col_ids_ref[at, :] == row_ids) & before
+        same = (jnp.concatenate([turned] * (samples // LANES), axis=1) == named) & before
         rank += jnp.sum(jnp.where(same, 1, 0), axis=0, keepdims=True)
-    owner = row_ids // FOLD_DEV
-    place = (row_ids % FOLD_DEV) * SLOTS + rank
+    place_ref[...] = (ids // FOLD_DEV) * SPOTS + (ids % FOLD_DEV) * SLOTS + rank
+    copy_ref[...] = dirs_ref[...]
+
+
+def scatter_body(devices, shares_ref, dirs_ref, ridge_ref, place_ref, image_ref, send_ref):
+    samples = dirs_ref.shape[1]
+    dirs = dirs_ref[...]
+    square = (RIDGE, RIDGE)
+    diagonal = lax.broadcasted_iota(jnp.int32, square, 0) == lax.broadcasted_iota(jnp.int32, square, 1)
+    ridge = jnp.sum(jnp.where(diagonal, ridge_ref[...], 0.0), axis=1, keepdims=True)
+    image = jnp.sum(shares_ref[...], axis=0) + ridge * dirs
+    image_ref[...] = image
     pieces = thirds(jnp.concatenate([dirs, image], axis=0))
     rest = jnp.zeros((LANES - 6 * RIDGE, samples), jnp.float32)
     stacked = jnp.concatenate([*pieces, rest], axis=0)
     turned = [stacked[:, group * LANES : (group + 1) * LANES].T for group in range(samples // LANES)]
     turned = jnp.concatenate(turned, axis=0).astype(jnp.bfloat16)
-    device = lax.broadcasted_iota(jnp.int32, (devices, samples), 0)
+    spot = place_ref[...] - SPOTS * lax.broadcasted_iota(jnp.int32, (devices, samples), 0)
     for quad in range(FOLD_DEV * SLOTS // 4):
         found = []
         for slot in range(4 * quad, 4 * quad + 4):
-            chosen = jnp.where((device == owner) & (place == slot), 1.0, 0.0).astype(jnp.bfloat16)
+            chosen = jnp.where(spot == slot, 1.0, 0.0).astype(jnp.bfloat16)
             parts = jnp.dot(chosen, turned, preferred_element_type=jnp.float32)
             found.append(parts[:, :32] + parts[:, 32:64] + parts[:, 64:96])
         send_ref[:, 0, quad * LANES : (quad + 1) * LANES] = jnp.concatenate(found, axis=1)
@@ -230,19 +268,36 @@
     devices = blk_count * row_count
     points = observation_points.T
     dirs = search_vectors.T
-    panel = jnp.concatenate([points, dirs.astype(jnp.bfloat16)], axis=0)
+    panel = lax.optimization_barrier(jnp.concatenate([points, dirs.astype(jnp.bfloat16)], axis=0))
+    points = panel[:FEAT]
+    swap = [(place, place ^ 1) for place in range(blk_count)]
+    pairs = blk_count // 2
     rows_of = lax.all_to_all(jnp.broadcast_to(points, (row_count, *points.shape)), "rows", 0, 0, tiled=True)
-    pairs = blk_count // 2
+    partner = lax.ppermute(panel, "blk", swap)
+    place, dirs = pl.pallas_call(
+        place_body,
+        out_shape=[
+            jax.ShapeDtypeStruct((1, samples), jnp.int32),
+            jax.ShapeDtypeStruct(dirs.shape, jnp.float32),
+        ],
+        name="places",
+    )(holdout_group.T, dirs)
+    to_pairs = jnp.broadcast_to(panel, (pairs, *panel.shape))
+    rows_of, to_pairs, place, dirs = lax.optimization_barrier((rows_of, to_pairs, place, dirs))
     columns_of = lax.all_to_all(
-        jnp.broadcast_to(panel, (pairs, *panel.shape)),
+        to_pairs,
         "blk",
         0,
         0,
         tiled=True,
         axis_index_groups=[[2 * pair + core for pair in range(pairs)] for core in range(2)],
     )
-    more_columns = lax.ppermute(columns_of, "blk", [(place, place ^ 1) for place in range(blk_count)])
-    shares = lax.all_to_all(apply_kernel(rows_of, columns_of, more_columns), "rows", 0, 0, tiled=True)
+    near = apply_kernel(rows_of, panel[None], partner[None])
+    near, columns_of = lax.optimization_barrier((near, columns_of))
+    more_columns = lax.ppermute(columns_of, "blk", swap)
+    own = (lax.axis_index("blk") // 2).astype(jnp.int32)[None]
+    shares = apply_kernel(rows_of, columns_of, more_columns, own, near, partner)
+    shares = lax.all_to_all(shares, "rows", 0, 0, tiled=True)
     image, send = pl.pallas_call(
         functools.partial(scatter_body, devices),
         out_shape=[
@@ -251,7 +306,7 @@
         ],
         compiler_params=pltpu.CompilerParams(vmem_limit_bytes=40 * 2**20),
         name="image_and_slots",
-    )(shares, dirs, shrinkage_levels[:, None], holdout_group.T, holdout_group)
+    )(shares, dirs, shrinkage_levels[None], place)
     received = lax.all_to_all(send, ("blk", "rows"), 0, 0, tiled=True)
     folds = pl.pallas_call(
         functools.partial(fold_body, FOLD_DEV / samples),

time: 121 us -> 119 us (0.983)
  blocking collectives: 47.7 us -> 28.5 us
  starting transfers between devices: 6.01 us -> 18 us
  Pallas kernels: 59.1 us -> 61.6 us
  waiting for transfers between devices: 5.12 us -> 6.4 us
    all_to_all x2 -> x1, blocking collectives: 31.1 us -> 11.3 us  [body(): shares = lax.all_to_all(shares, 'rows', 0, 0, tiled=True)]
    all_to_all x1 -> x2, starting transfers between devices: 3.73 us -> 13.1 us  [the longest x1 6.79 us: body(): lax.all_to_all(jnp.broadcast_to(points, (row_count, *points.shape)), 'row...]
    pallas_call x1 -> x3, Pallas kernels: 55.8 us -> 58.4 us  [the longest x2 56.8 us: apply_kernel(): pl.pallas_call(functools.partial(apply_body, skip), out_shape=jax.ShapeDt...]
    ppermute x1 -> x2, starting transfers between devices: 2.28 us -> 4.86 us  [the longest x1 3.91 us: body(): more_columns = lax.ppermute(columns_of, 'blk', swap)]
    ppermute x1 -> x2, waiting for transfers between devices: 0.01 us -> 1.63 us  [the longest x1 1.63 us: body(): more_columns = lax.ppermute(columns_of, 'blk', swap)]
    all_to_all x1 -> x2, waiting for transfers between devices: 5.12 us -> 4.76 us  [the longest x1 4.19 us: body(): lax.all_to_all(jnp.broadcast_to(points, (row_count, *points.shape)), 'row...]
  transfers between devices with their start and end apart: 2 -> 4, of which waited for: 1 -> 3; matrix products, arithmetic and copies ran while one was open for 0% -> 1% of each run, Pallas kernels for 0% -> 9%
where the time goes in v3:
time: 119 us; the launch traced here: 118 us
  Pallas kernels  61.6 us (52%)
  blocking collectives  28.5 us (24%)
  starting transfers between devices  18 us (15%)
  waiting for transfers between devices  6.4 us (5%)
  local copies, waits for them, and re-layouts  2.29 us (2%)
    pallas_call x2, Pallas kernels, apply_kernel(): pl.pallas_call(functools.partial(apply_body, skip), out_shape=jax.ShapeDt...  56.8 us
    all_to_all x1, blocking collectives, body(): received = lax.all_to_all(send, ('blk', 'rows'), 0, 0, tiled=True)  17.2 us
    all_to_all x1, blocking collectives, body(): shares = lax.all_to_all(shares, 'rows', 0, 0, tiled=True)  11.3 us
    all_to_all x1, starting transfers between devices, body(): lax.all_to_all(jnp.broadcast_to(points, (row_count, *points.shape)), 'row...  6.79 us
    all_to_all x1, starting transfers between devices, body(): lax.all_to_all(to_pairs, 'blk', 0, 0, tiled=True, axis_index_groups=[[2 *...  6.36 us
    all_to_all x1, waiting for transfers between devices, body(): lax.all_to_all(jnp.broadcast_to(points, (row_count, *points.shape)), 'row...  4.19 us
    ppermute x1, starting transfers between devices, body(): more_columns = lax.ppermute(columns_of, 'blk', swap)  3.91 us
  transfers between devices with their start and end apart: 4, of which 3 were waited for; matrix products, arithmetic and copies ran while one was open for 1% of the time, Pallas kernels for 9%

profile of v3, /device:TPU:1, one launch (start us, length us, event | category | flops | bytes accessed | tf_op | source)
XLA Modules:
  0.0 118.2 jit_solution(9276704792063125409)
XLA Ops:
  0.6 0.0 copy-start.3
  0.6 0.8 bitcast_convert_fusion
  1.5 0.0 copy-done.3
  1.5 0.8 broadcast_in_dim.19
  2.3 6.8 %all-to-all-start = ((bf16[8,32,768]{2,1,0:T(8,128)(2,1)}), bf16[8,32,768]{2,1,0:T(8,128)(2,1)S(1)}, u32[]{:S(2)}, u32[]{:S(2)}) async-start(bf16[8,32,768]{2,1,0:T(8,128)(2,1)} %broadcast_in_dim.19), calls=%async_computation | async-start | bytes 786432 | tf_op jit(solution)/shard_map/all_to_all | solution.py:275
  9.0 1.0 collective-permute-start
  10.0 1.7 %places.1 = (s32[1,768]{1,0:T(1,128)}, f32[16,768]{1,0:T(8,128)}) custom-call(s32[1,768]{1,0:T(1,128)} %bitcast.14, f32[16,768]{1,0:T(8,128)} %bitcast.12), custom_call_target="tpu_custom_call" | custom-call | tf_op jit(solution)/shard_map/places/pallas_call | solution.py:277
  11.7 4.2 %all-to-all-done.refs_0_.refs_3_ = bf16[8,32,768]{2,1,0:T(8,128)(2,1)S(1)} async-done(((bf16[8,32,768]{2,1,0:T(8,128)(2,1)}), bf16[8,32,768]{2,1,0:T(8,128)(2,1)S(1)}, u32[]{:S(2)}, u32[]{:S(2)}) %all-to-all-start) | async-done | bytes 393248 | tf_op jit(solution)/shard_map/all_to_all | solution.py:275
  15.8 0.8 broadcast_in_dim.20
  16.7 6.4 %all-to-all-start.1 = ((bf16[8,48,768]{2,1,0:T(8,128)(2,1)}), bf16[8,48,768]{2,1,0:T(8,128)(2,1)S(1)}, u32[]{:S(2)}, u32[]{:S(2)}) async-start(bf16[8,48,768]{2,1,0:T(8,128)(2,1)} %broadcast_in_dim.20), calls=%async_computation.1 | async-start | bytes 1179648 | tf_op jit(solution)/shard_map/all_to_all | solution.py:287
  23.1 0.0 collective-permute-done.refs_2_
  23.1 8.9 %kernel_rows.1.refs_1_ = f32[8,16,768]{2,1,0:T(8,128)S(1)} custom-call(bf16[8,32,768]{2,1,0:T(8,128)(2,1)S(1)} %all-to-all-done.refs_0_.refs_3_, bf16[1,48,768]{2,1,0:T(8,128)(2,1)S(1)} %bitcast.9, bf16[1,48,768]{2,1,0:T(8,128)(2,1)S(1)} %bitcast.11), custom_call_target="tpu_custom_call" | custom-call | flops 5637144576 | bytes 3145728 | tf_op jit(solution)/shard_map/kernel_rows/pallas_call | solution.py:189
  32.0 0.6 all-to-all-done.1.refs_4_
  32.6 3.9 %collective-permute-start.1 = (bf16[8,48,768]{2,1,0:T(8,128)(2,1)S(1)}, bf16[8,48,768]{2,1,0:T(8,128)(2,1)S(1)}, u32[]{:S(2)}, u32[]{:S(2)}) collective-permute-start(bf16[8,48,768]{2,1,0:T(8,128)(2,1)S(1)} %all-to-all-done.1.refs_4_), channel_id=1, source_target_pairs={{0,8},{8,0},{16,24},{24,16},{32,40},{40,32},{48,56},{56,48},{64,72... | collective-permute-start | bytes 1769480 | tf_op jit(solution)/shard_map/ppermute | solution.py:297
  36.5 1.6 %collective-permute-done.1.refs_5_ = bf16[8,48,768]{2,1,0:T(8,128)(2,1)S(1)} collective-permute-done((bf16[8,48,768]{2,1,0:T(8,128)(2,1)S(1)}, bf16[8,48,768]{2,1,0:T(8,128)(2,1)S(1)}, u32[]{:S(2)}, u32[]{:S(2)}) %collective-permute-start.1) | collective-permute-done | bytes 589856 | tf_op jit(solution)/shard_map/ppermute | solution.py:297
  38.1 0.0 copy-start.1
  38.1 47.8 %kernel_rows_rest.1 = f32[8,16,768]{2,1,0:T(8,128)S(1)} custom-call(s32[1]{0:T(128)} %bitcast.refs_0_, f32[8,16,768]{2,1,0:T(8,128)S(1)} %kernel_rows.1.refs_1_, bf16[48,768]{1,0:T(8,128)(2,1)S(1)} %collective-permute-done.refs_2_, bf16[8,32,768]{2,1,0:T(8,128)(2,1)S(1)} %all-to-all-done.refs_0_.refs_3_, bf16[8,48,768]{2,1,0:T(8,128)(2,1)S(1)} %all-to-all-done.1.refs_4_, ...), custom_call_target="tpu_custom_call" | custom-call | flops 40265318400 | bytes 3145728 | tf_op jit(solution)/shard_map/kernel_rows_rest/pallas_call | solution.py:189
  85.9 0.0 copy-start
  85.9 11.3 %all_to_all.20.shares_ref = f32[8,16,768]{2,1,0:T(8,128)S(1)} all-to-all(f32[8,16,768]{2,1,0:T(8,128)S(1)} %kernel_rows_rest.1), channel_id=1, replica_groups=mesh['blk'=16,'rows'=8] {'rows'}, dimensions={0} | all-to-all | bytes 786432 | tf_op jit(solution)/shard_map/all_to_all | solution.py:300
  97.2 0.0 copy-start.2
  97.2 0.0 copy-done.1
  97.2 0.0 copy-done
  97.2 0.6 copy-done.2
  97.9 1.7 %image_and_slots.1 = (f32[16,768]{1,0:T(8,128)}, f32[128,1,384]{2,1,0:T(1,128)S(1)}) custom-call(f32[8,16,768]{2,1,0:T(8,128)S(1)} %all_to_all.20.shares_ref, f32[16,768]{1,0:T(8,128)S(1)} %copy-done, f32[1,16]{1,0:T(1,128)S(1)} %bitcast.10, s32[1,768]{1,0:T(1,128)S(1)} %copy-done.1), custom_call_target="tpu_custom_call" | custom-call | tf_op jit(solution)/shard_map/image_and_slots/pallas_call | solution.py:301
  99.6 17.2 %all_to_all.21.rows_ref = f32[128,1,384]{2,1,0:T(1,128)S(1)} all-to-all(f32[128,1,384]{2,1,0:T(1,128)S(1)} %get-tuple-element.21), channel_id=1, replica_groups=mesh['blk'=16,'rows'=8] {'blk','rows'}, dimensions={0} | all-to-all | bytes 393216 | tf_op jit(solution)/shard_map/all_to_all | solution.py:310
  116.8 1.4 %fold_products.1 = f32[4,256]{1,0:T(4,128)} custom-call(f32[128,1,384]{2,1,0:T(1,128)S(1)} %all_to_all.21.rows_ref), custom_call_target="tpu_custom_call" | custom-call | tf_op jit(solution)/shard_map/fold_products/pallas_call | solution.py:311
  (2 shorter events, 0.0 us)
Async XLA Ops:
  0.6 0.8 copy-start.3
  2.3 13.6 %all-to-all-start = ((bf16[8,32,768]{2,1,0:T(8,128)(2,1)}), bf16[8,32,768]{2,1,0:T(8,128)(2,1)S(1)}, u32[]{:S(2)}, u32[]{:S(2)}) async-start(bf16[8,32,768]{2,1,0:T(8,128)(2,1)} %broadcast_in_dim.19), calls=%async_computation | async-start | bytes 786432 | tf_op jit(solution)/shard_map/all_to_all | solution.py:275
  9.0 14.0 %collective-permute-start = (bf16[48,768]{1,0:T(8,128)(2,1)S(1)}, bf16[48,768]{1,0:T(8,128)(2,1)S(1)}, u32[]{:S(2)}, u32[]{:S(2)}) collective-permute-start(bf16[48,768]{1,0:T(8,128)(2,1)S(1)} %pad_maximum_fusion), channel_id=1, source_target_pairs={{0,8},{8,0},{16,24},{24,16},{32,40},{40,32},{48,56},{56,48},{64,72... | collective-permute-start | bytes 221192 | tf_op jit(solution)/shard_map/ppermute | solution.py:276
  16.7 15.9 %all-to-all-start.1 = ((bf16[8,48,768]{2,1,0:T(8,128)(2,1)}), bf16[8,48,768]{2,1,0:T(8,128)(2,1)S(1)}, u32[]{:S(2)}, u32[]{:S(2)}) async-start(bf16[8,48,768]{2,1,0:T(8,128)(2,1)} %broadcast_in_dim.20), calls=%async_computation.1 | async-start | bytes 1179648 | tf_op jit(solution)/shard_map/all_to_all | solution.py:287
  32.6 5.5 %collective-permute-start.1 = (bf16[8,48,768]{2,1,0:T(8,128)(2,1)S(1)}, bf16[8,48,768]{2,1,0:T(8,128)(2,1)S(1)}, u32[]{:S(2)}, u32[]{:S(2)}) collective-permute-start(bf16[8,48,768]{2,1,0:T(8,128)(2,1)S(1)} %all-to-all-done.1.refs_4_), channel_id=1, source_target_pairs={{0,8},{8,0},{16,24},{24,16},{32,40},{40,32},{48,56},{56,48},{64,72... | collective-permute-start | bytes 1769480 | tf_op jit(solution)/shard_map/ppermute | solution.py:297
  38.1 59.1 %copy-start.1 = (s32[1,768]{1,0:T(1,128)S(1)}, s32[1,768]{1,0:T(1,128)}, u32[]{:S(2)}) copy-start(s32[1,768]{1,0:T(1,128)} %get-tuple-element.19.place_ref) | copy-start | bytes 9220
  85.9 11.3 %copy-start = (f32[16,768]{1,0:T(8,128)S(1)}, f32[16,768]{1,0:T(8,128)}, u32[]{:S(2)}) copy-start(f32[16,768]{1,0:T(8,128)} %get-tuple-element.18.dirs_ref) | copy-start | bytes 147460
  97.2 0.7 copy-start.2

commit v4 on v3

--- a/solution.py
+++ b/solution.py
@@ -205,7 +205,14 @@
     )(*([own, before, near] if skip else []), rows_of, columns_of, more_columns)
 
 
-def place_body(ids_ref, dirs_ref, place_ref, copy_ref):
+def panel_body(points_ref, dirs_ref, panel_ref, to_rows_ref):
+    points = points_ref[...]
+    panel_ref[...] = jnp.concatenate([points, dirs_ref[...].astype(jnp.bfloat16)], axis=0)
+    for device in range(to_rows_ref.shape[0]):
+        to_rows_ref[device] = points
+
+
+def place_body(ids_ref, dirs_ref, ridge_ref, panel_ref, place_ref, copy_ref, ridged_ref, own_ref, to_pairs_ref):
     ids = ids_ref[...]
     samples = ids.shape[1]
     named = ids.astype(jnp.float32)
@@ -218,16 +225,20 @@
         same = (jnp.concatenate([turned] * (samples // LANES), axis=1) == named) & before
         rank += jnp.sum(jnp.where(same, 1, 0), axis=0, keepdims=True)
     place_ref[...] = (ids // FOLD_DEV) * SPOTS + (ids % FOLD_DEV) * SLOTS + rank
-    copy_ref[...] = dirs_ref[...]
-
-
-def scatter_body(devices, shares_ref, dirs_ref, ridge_ref, place_ref, image_ref, send_ref):
-    samples = dirs_ref.shape[1]
     dirs = dirs_ref[...]
     square = (RIDGE, RIDGE)
     diagonal = lax.broadcasted_iota(jnp.int32, square, 0) == lax.broadcasted_iota(jnp.int32, square, 1)
-    ridge = jnp.sum(jnp.where(diagonal, ridge_ref[...], 0.0), axis=1, keepdims=True)
-    image = jnp.sum(shares_ref[...], axis=0) + ridge * dirs
+    copy_ref[...] = dirs
+    ridged_ref[...] = jnp.sum(jnp.where(diagonal, ridge_ref[...], 0.0), axis=1, keepdims=True) * dirs
+    own_ref[0] = panel_ref[...]
+    for device in range(to_pairs_ref.shape[0]):
+        to_pairs_ref[device] = panel_ref[...]
+
+
+def scatter_body(devices, shares_ref, dirs_ref, ridged_ref, place_ref, image_ref, send_ref):
+    samples = dirs_ref.shape[1]
+    dirs = dirs_ref[...]
+    image = jnp.sum(shares_ref[...], axis=0) + ridged_ref[...]
     image_ref[...] = image
     pieces = thirds(jnp.concatenate([dirs, image], axis=0))
     rest = jnp.zeros((LANES - 6 * RIDGE, samples), jnp.float32)
@@ -266,24 +277,33 @@
     samples = observation_points.shape[0]
     blk_count, row_count = lax.axis_size("blk"), lax.axis_size("rows")
     devices = blk_count * row_count
-    points = observation_points.T
+    pairs = blk_count // 2
+    swap = [(place, place ^ 1) for place in range(blk_count)]
     dirs = search_vectors.T
-    panel = lax.optimization_barrier(jnp.concatenate([points, dirs.astype(jnp.bfloat16)], axis=0))
-    points = panel[:FEAT]
-    swap = [(place, place ^ 1) for place in range(blk_count)]
-    pairs = blk_count // 2
-    rows_of = lax.all_to_all(jnp.broadcast_to(points, (row_count, *points.shape)), "rows", 0, 0, tiled=True)
+    panel, to_rows = pl.pallas_call(
+        panel_body,
+        out_shape=[
+            jax.ShapeDtypeStruct((FEAT + RIDGE, samples), jnp.bfloat16),
+            jax.ShapeDtypeStruct((row_count, FEAT, samples), jnp.bfloat16),
+        ],
+        name="panels",
+    )(observation_points.T, dirs)
+    rows_of = lax.all_to_all(to_rows, "rows", 0, 0, tiled=True)
     partner = lax.ppermute(panel, "blk", swap)
-    place, dirs = pl.pallas_call(
+    place, dirs, ridged, own_panel, to_pairs = pl.pallas_call(
         place_body,
         out_shape=[
-            jax.ShapeDtypeStruct((1, samples), jnp.int32),
-            jax.ShapeDtypeStruct(dirs.shape, jnp.float32),
+            pltpu.VMEM((1, samples), jnp.int32),
+            pltpu.VMEM(dirs.shape, jnp.float32),
+            pltpu.VMEM(dirs.shape, jnp.float32),
+            pltpu.VMEM((1, *panel.shape), jnp.bfloat16),
+            jax.ShapeDtypeStruct((pairs, *panel.shape), jnp.bfloat16),
         ],
         name="places",
-    )(holdout_group.T, dirs)
-    to_pairs = jnp.broadcast_to(panel, (pairs, *panel.shape))
-    rows_of, to_pairs, place, dirs = lax.optimization_barrier((rows_of, to_pairs, place, dirs))
+    )(holdout_group.T, dirs, shrinkage_levels[None], panel)
+    rows_of, to_pairs, own_panel, place, dirs, ridged = lax.optimization_barrier(
+        (rows_of, to_pairs, own_panel, place, dirs, ridged)
+    )
     columns_of = lax.all_to_all(
         to_pairs,
         "blk",
@@ -292,7 +312,7 @@
         tiled=True,
         axis_index_groups=[[2 * pair + core for pair in range(pairs)] for core in range(2)],
     )
-    near = apply_kernel(rows_of, panel[None], partner[None])
+    near = apply_kernel(rows_of, own_panel, partner[None])
     near, columns_of = lax.optimization_barrier((near, columns_of))
     more_columns = lax.ppermute(columns_of, "blk", swap)
     own = (lax.axis_index("blk") // 2).astype(jnp.int32)[None]
@@ -306,7 +326,7 @@
         ],
         compiler_params=pltpu.CompilerParams(vmem_limit_bytes=40 * 2**20),
         name="image_and_slots",
-    )(shares, dirs, shrinkage_levels[None], place)
+    )(shares, dirs, ridged, place)
     received = lax.all_to_all(send, ("blk", "rows"), 0, 0, tiled=True)
     folds = pl.pallas_call(
         functools.partial(fold_body, FOLD_DEV / samples),

time: 119 us -> 117 us (0.983)
  local copies, waits for them, and re-layouts: 2.29 us -> 0.01 us
  Pallas kernels: 61.6 us -> 63.5 us
    pallas_call x1 -> x2, Pallas kernels: 1.66 us -> 3.62 us  [the longest x1 2 us: body(): pl.pallas_call(place_body, out_shape=[pltpu.VMEM((1, samples), jnp.int32)...]
    broadcast_in_dim x2 -> x0, local copies, waits for them, and re-layouts: 1.62 us -> none  [the longest x1 0.85 us: body(): to_pairs = jnp.broadcast_to(panel, (pairs, *panel.shape))]
  transfers between devices with their start and end apart: 4 -> 4, of which waited for: 3 -> 3; matrix products, arithmetic and copies ran while one was open for 1% -> 0% of each run, Pallas kernels for 9% -> 9%
where the time goes in v4:
time: 117 us
  Pallas kernels  63.5 us (54%)
  blocking collectives  28.4 us (24%)
  starting transfers between devices  18.2 us (16%)
  waiting for transfers between devices  5.96 us (5%)
    pallas_call x2, Pallas kernels, apply_kernel(): pl.pallas_call(functools.partial(apply_body, skip), out_shape=jax.ShapeDt...  56.8 us
    all_to_all x1, blocking collectives, body(): received = lax.all_to_all(send, ('blk', 'rows'), 0, 0, tiled=True)  17.2 us
    all_to_all x1, blocking collectives, body(): shares = lax.all_to_all(shares, 'rows', 0, 0, tiled=True)  11.2 us
    all_to_all x1, starting transfers between devices, body(): rows_of = lax.all_to_all(to_rows, 'rows', 0, 0, tiled=True)  6.92 us
    all_to_all x1, starting transfers between devices, body(): lax.all_to_all(to_pairs, 'blk', 0, 0, tiled=True, axis_index_groups=[[2 *...  6.36 us
    ppermute x1, starting transfers between devices, body(): more_columns = lax.ppermute(columns_of, 'blk', swap)  3.91 us
    all_to_all x1, waiting for transfers between devices, body(): rows_of = lax.all_to_all(to_rows, 'rows', 0, 0, tiled=True)  3.76 us
  transfers between devices with their start and end apart: 4, of which 3 were waited for; matrix products, arithmetic and copies ran while one was open for 0% of the time, Pallas kernels for 9%

profile of v4, /device:TPU:1, one launch (start us, length us, event | category | flops | bytes accessed | tf_op | source)
XLA Modules:
  0.0 116.7 jit_solution(4282474750597088852)
XLA Ops:
  0.6 1.6 %panels.1 = (bf16[48,768]{1,0:T(8,128)(2,1)}, bf16[8,32,768]{2,1,0:T(8,128)(2,1)}) custom-call(bf16[32,768]{1,0:T(8,128)(2,1)} %bitcast.10, f32[16,768]{1,0:T(8,128)} %bitcast.8), custom_call_target="tpu_custom_call" | custom-call | tf_op jit(solution)/shard_map/panels/pallas_call | solution.py:283
  2.2 0.0 copy-start
  2.2 6.9 %all-to-all-start = ((bf16[8,32,768]{2,1,0:T(8,128)(2,1)}), bf16[8,32,768]{2,1,0:T(8,128)(2,1)S(1)}, u32[]{:S(2)}, u32[]{:S(2)}) async-start(bf16[8,32,768]{2,1,0:T(8,128)(2,1)} %get-tuple-element.19), calls=%async_computation | async-start | bytes 786432 | tf_op jit(solution)/shard_map/all_to_all | solution.py:291
  9.2 0.0 copy-done
  9.2 1.0 collective-permute-start
  10.2 2.0 %places.1 = (s32[1,768]{1,0:T(1,128)S(1)}, f32[16,768]{1,0:T(8,128)S(1)}, f32[16,768]{1,0:T(8,128)S(1)}, bf16[1,48,768]{2,1,0:T(8,128)(2,1)S(1)}, bf16[8,48,768]{2,1,0:T(8,128)(2,1)}) custom-call(s32[1,768]{1,0:T(1,128)} %bitcast.11, f32[16,768]{1,0:T(8,128)} %bitcast.9, f32[1,16]{1,0:T(1,128)} %bitcast.12, bf16[48,768]{1,0:T(8,128)(2,1)} %get-tuple-element.20.panel_ref), custom_call_target="tpu_custom_call" | custom-call | tf_op jit(solution)/shard_map/places/pallas_call | solution.py:293
  12.2 3.8 %all-to-all-done.refs_0_.refs_3_ = bf16[8,32,768]{2,1,0:T(8,128)(2,1)S(1)} async-done(((bf16[8,32,768]{2,1,0:T(8,128)(2,1)}), bf16[8,32,768]{2,1,0:T(8,128)(2,1)S(1)}, u32[]{:S(2)}, u32[]{:S(2)}) %all-to-all-start) | async-done | bytes 393248 | tf_op jit(solution)/shard_map/all_to_all | solution.py:291
  16.0 6.4 %all-to-all-start.1 = ((bf16[8,48,768]{2,1,0:T(8,128)(2,1)}), bf16[8,48,768]{2,1,0:T(8,128)(2,1)S(1)}, u32[]{:S(2)}, u32[]{:S(2)}) async-start(bf16[8,48,768]{2,1,0:T(8,128)(2,1)} %get-tuple-element.28), calls=%async_computation.1 | async-start | bytes 1179648 | tf_op jit(solution)/shard_map/all_to_all | solution.py:307
  22.3 0.0 collective-permute-done.refs_2_
  22.3 9.0 %kernel_rows.1.refs_1_ = f32[8,16,768]{2,1,0:T(8,128)S(1)} custom-call(bf16[8,32,768]{2,1,0:T(8,128)(2,1)S(1)} %all-to-all-done.refs_0_.refs_3_, bf16[1,48,768]{2,1,0:T(8,128)(2,1)S(1)} %get-tuple-element.27.refs_1_, bf16[1,48,768]{2,1,0:T(8,128)(2,1)S(1)} %bitcast.7), custom_call_target="tpu_custom_call" | custom-call | flops 5637144576 | bytes 3145728 | tf_op jit(solution)/shard_map/kernel_rows/pallas_call | solution.py:189
  31.3 0.6 all-to-all-done.1.refs_4_
  31.9 3.9 %collective-permute-start.1 = (bf16[8,48,768]{2,1,0:T(8,128)(2,1)S(1)}, bf16[8,48,768]{2,1,0:T(8,128)(2,1)S(1)}, u32[]{:S(2)}, u32[]{:S(2)}) collective-permute-start(bf16[8,48,768]{2,1,0:T(8,128)(2,1)S(1)} %all-to-all-done.1.refs_4_), channel_id=1, source_target_pairs={{0,8},{8,0},{16,24},{24,16},{32,40},{40,32},{48,56},{56,48},{64,72... | collective-permute-start | bytes 1769480 | tf_op jit(solution)/shard_map/ppermute | solution.py:317
  35.8 1.6 %collective-permute-done.1.refs_5_ = bf16[8,48,768]{2,1,0:T(8,128)(2,1)S(1)} collective-permute-done((bf16[8,48,768]{2,1,0:T(8,128)(2,1)S(1)}, bf16[8,48,768]{2,1,0:T(8,128)(2,1)S(1)}, u32[]{:S(2)}, u32[]{:S(2)}) %collective-permute-start.1) | collective-permute-done | bytes 589856 | tf_op jit(solution)/shard_map/ppermute | solution.py:317
  37.4 47.8 %kernel_rows_rest.1 = f32[8,16,768]{2,1,0:T(8,128)S(1)} custom-call(s32[1]{0:T(128)} %bitcast.refs_0_, f32[8,16,768]{2,1,0:T(8,128)S(1)} %kernel_rows.1.refs_1_, bf16[48,768]{1,0:T(8,128)(2,1)S(1)} %collective-permute-done.refs_2_, bf16[8,32,768]{2,1,0:T(8,128)(2,1)S(1)} %all-to-all-done.refs_0_.refs_3_, bf16[8,48,768]{2,1,0:T(8,128)(2,1)S(1)} %all-to-all-done.1.refs_4_, ...), custom_call_target="tpu_custom_call" | custom-call | flops 40265318400 | bytes 3145728 | tf_op jit(solution)/shard_map/kernel_rows_rest/pallas_call | solution.py:189
  85.2 11.2 %all_to_all.20.shares_ref = f32[8,16,768]{2,1,0:T(8,128)S(1)} all-to-all(f32[8,16,768]{2,1,0:T(8,128)S(1)} %kernel_rows_rest.1), channel_id=1, replica_groups=mesh['blk'=16,'rows'=8] {'rows'}, dimensions={0} | all-to-all | bytes 786432 | tf_op jit(solution)/shard_map/all_to_all | solution.py:320
  96.5 1.7 %image_and_slots.1 = (f32[16,768]{1,0:T(8,128)}, f32[128,1,384]{2,1,0:T(1,128)S(1)}) custom-call(f32[8,16,768]{2,1,0:T(8,128)S(1)} %all_to_all.20.shares_ref, f32[16,768]{1,0:T(8,128)S(1)} %get-tuple-element.31.dirs_ref, f32[16,768]{1,0:T(8,128)S(1)} %get-tuple-element.32.ridged_ref, s32[1,768]{1,0:T(1,128)S(1)} %get-tuple-element.33.place_ref), custom_call_target="tpu_custom_call" | custom-call | tf_op jit(solution)/shard_map/image_and_slots/pallas_call | solution.py:321
  98.1 17.2 %all_to_all.21.rows_ref = f32[128,1,384]{2,1,0:T(1,128)S(1)} all-to-all(f32[128,1,384]{2,1,0:T(1,128)S(1)} %get-tuple-element.35), channel_id=1, replica_groups=mesh['blk'=16,'rows'=8] {'blk','rows'}, dimensions={0} | all-to-all | bytes 393216 | tf_op jit(solution)/shard_map/all_to_all | solution.py:330
  115.3 1.4 %fold_products.1 = f32[4,256]{1,0:T(4,128)} custom-call(f32[128,1,384]{2,1,0:T(1,128)S(1)} %all_to_all.21.rows_ref), custom_call_target="tpu_custom_call" | custom-call | tf_op jit(solution)/shard_map/fold_products/pallas_call | solution.py:331
Async XLA Ops:
  2.2 6.9 %copy-start = (bf16[48,768]{1,0:T(8,128)(2,1)S(1)}, bf16[48,768]{1,0:T(8,128)(2,1)}, u32[]{:S(2)}) copy-start(bf16[48,768]{1,0:T(8,128)(2,1)} %get-tuple-element.20.panel_ref) | copy-start | bytes 221188
  2.2 13.7 %all-to-all-start = ((bf16[8,32,768]{2,1,0:T(8,128)(2,1)}), bf16[8,32,768]{2,1,0:T(8,128)(2,1)S(1)}, u32[]{:S(2)}, u32[]{:S(2)}) async-start(bf16[8,32,768]{2,1,0:T(8,128)(2,1)} %get-tuple-element.19), calls=%async_computation | async-start | bytes 786432 | tf_op jit(solution)/shard_map/all_to_all | solution.py:291
  9.2 13.2 %collective-permute-start = (bf16[48,768]{1,0:T(8,128)(2,1)S(1)}, bf16[48,768]{1,0:T(8,128)(2,1)S(1)}, u32[]{:S(2)}, u32[]{:S(2)}) collective-permute-start(bf16[48,768]{1,0:T(8,128)(2,1)S(1)} %copy-done), channel_id=1, source_target_pairs={{0,8},{8,0},{16,24},{24,16},{32,40},{40,32},{48,56},{56,48},{64,72... | collective-permute-start | bytes 221192 | tf_op jit(solution)/shard_map/ppermute | solution.py:292
  16.0 15.9 %all-to-all-start.1 = ((bf16[8,48,768]{2,1,0:T(8,128)(2,1)}), bf16[8,48,768]{2,1,0:T(8,128)(2,1)S(1)}, u32[]{:S(2)}, u32[]{:S(2)}) async-start(bf16[8,48,768]{2,1,0:T(8,128)(2,1)} %get-tuple-element.28), calls=%async_computation.1 | async-start | bytes 1179648 | tf_op jit(solution)/shard_map/all_to_all | solution.py:307
  31.9 5.5 %collective-permute-start.1 = (bf16[8,48,768]{2,1,0:T(8,128)(2,1)S(1)}, bf16[8,48,768]{2,1,0:T(8,128)(2,1)S(1)}, u32[]{:S(2)}, u32[]{:S(2)}) collective-permute-start(bf16[8,48,768]{2,1,0:T(8,128)(2,1)S(1)} %all-to-all-done.1.refs_4_), channel_id=1, source_target_pairs={{0,8},{8,0},{16,24},{24,16},{32,40},{40,32},{48,56},{56,48},{64,72... | collective-permute-start | bytes 1769480 | tf_op jit(solution)/shard_map/ppermute | solution.py:317

commit v5 on v4

--- a/solution.py
+++ b/solution.py
@@ -68,11 +68,11 @@
             at = pl.ds(pl.multiple_of(block * span + group * LANES, LANES), LANES)
             feats[at, :] = turned
             held[at, :LANES] = turned
+            held[at, LANES:] = jnp.zeros((LANES, LANES), jnp.bfloat16)
+            total[at, :] = jnp.zeros((LANES, LANES), jnp.float32)
         return carry
 
     lax.fori_loop(0, blocks_a, fill_a, 0)
-    held[:, LANES:] = jnp.zeros((rows_a, LANES), jnp.bfloat16)
-    total[...] = jnp.zeros_like(total)
     columns[:, :LANES] = jnp.zeros((columns.shape[0], LANES), jnp.float32)
     past = columns.shape[1] - LANES - rows_b
     columns[:, LANES + rows_b :] = jnp.zeros((columns.shape[0], past), jnp.float32)
@@ -257,18 +257,15 @@
 
 def fold_body(scale, rows_ref, out_ref):
     rows = rows_ref[:, 0, :]
-    products = lax.dot_general(
-        rows,
-        rows,
-        (((0,), (0,)), ((), ())),
-        precision=lax.Precision.HIGHEST,
-        preferred_element_type=jnp.float32,
-    )
+    width = 2 * RIDGE
+    turned = rows.T
+    dirs = jnp.concatenate([turned[at : at + RIDGE] for at in range(0, turned.shape[0], width)], axis=0)
+    products = jnp.dot(dirs, rows, precision=lax.Precision.HIGHEST, preferred_element_type=jnp.float32)
     for fold in range(FOLD_DEV):
         found = jnp.zeros((RIDGE, RIDGE), jnp.float32)
         for slot in range(fold * SLOTS, (fold + 1) * SLOTS):
-            at = 2 * RIDGE * slot
-            found += products[at : at + RIDGE, at + RIDGE : at + 2 * RIDGE]
+            at = width * slot + RIDGE
+            found += products[slot * RIDGE : (slot + 1) * RIDGE, at : at + RIDGE]
         lines = [found[line : line + 1, :] for line in range(RIDGE)]
         out_ref[fold : fold + 1, :] = jnp.concatenate(lines, axis=1) * scale
 

time: 117 us -> 117 us (level)
  no operation moved by 1% of the time
where the time goes in v5:
time: 117 us; the launch traced here: 116 us
  Pallas kernels  63 us (54%)
  blocking collectives  28.3 us (24%)
  starting transfers between devices  18.2 us (16%)
  waiting for transfers between devices  6.02 us (5%)
    pallas_call x2, Pallas kernels, apply_kernel(): pl.pallas_call(functools.partial(apply_body, skip), out_shape=jax.ShapeDt...  56.5 us
    all_to_all x1, blocking collectives, body(): received = lax.all_to_all(send, ('blk', 'rows'), 0, 0, tiled=True)  17.1 us
    all_to_all x1, blocking collectives, body(): shares = lax.all_to_all(shares, 'rows', 0, 0, tiled=True)  11.2 us
    all_to_all x1, starting transfers between devices, body(): rows_of = lax.all_to_all(to_rows, 'rows', 0, 0, tiled=True)  6.92 us
    all_to_all x1, starting transfers between devices, body(): lax.all_to_all(to_pairs, 'blk', 0, 0, tiled=True, axis_index_groups=[[2 *...  6.36 us
    ppermute x1, starting transfers between devices, body(): more_columns = lax.ppermute(columns_of, 'blk', swap)  3.91 us
    all_to_all x1, waiting for transfers between devices, body(): rows_of = lax.all_to_all(to_rows, 'rows', 0, 0, tiled=True)  3.76 us
  transfers between devices with their start and end apart: 4, of which 3 were waited for; matrix products, arithmetic and copies ran while one was open for 0% of the time, Pallas kernels for 9%

profile of v5, /device:TPU:1, one launch (start us, length us, event | category | flops | bytes accessed | tf_op | source)
XLA Modules:
  0.0 116.2 jit_solution(8007003756170599143)
XLA Ops:
  0.6 1.6 %panels.1 = (bf16[48,768]{1,0:T(8,128)(2,1)}, bf16[8,32,768]{2,1,0:T(8,128)(2,1)}) custom-call(bf16[32,768]{1,0:T(8,128)(2,1)} %bitcast.10, f32[16,768]{1,0:T(8,128)} %bitcast.8), custom_call_target="tpu_custom_call" | custom-call | tf_op jit(solution)/shard_map/panels/pallas_call | solution.py:280
  2.2 0.0 copy-start
  2.2 6.9 %all-to-all-start = ((bf16[8,32,768]{2,1,0:T(8,128)(2,1)}), bf16[8,32,768]{2,1,0:T(8,128)(2,1)S(1)}, u32[]{:S(2)}, u32[]{:S(2)}) async-start(bf16[8,32,768]{2,1,0:T(8,128)(2,1)} %get-tuple-element.19), calls=%async_computation | async-start | bytes 786432 | tf_op jit(solution)/shard_map/all_to_all | solution.py:288
  9.2 0.0 copy-done
  9.2 1.0 collective-permute-start
  10.2 2.0 %places.1 = (s32[1,768]{1,0:T(1,128)S(1)}, f32[16,768]{1,0:T(8,128)S(1)}, f32[16,768]{1,0:T(8,128)S(1)}, bf16[1,48,768]{2,1,0:T(8,128)(2,1)S(1)}, bf16[8,48,768]{2,1,0:T(8,128)(2,1)}) custom-call(s32[1,768]{1,0:T(1,128)} %bitcast.11, f32[16,768]{1,0:T(8,128)} %bitcast.9, f32[1,16]{1,0:T(1,128)} %bitcast.12, bf16[48,768]{1,0:T(8,128)(2,1)} %get-tuple-element.20.panel_ref), custom_call_target="tpu_custom_call" | custom-call | tf_op jit(solution)/shard_map/places/pallas_call | solution.py:290
  12.2 3.8 %all-to-all-done.refs_0_.refs_3_ = bf16[8,32,768]{2,1,0:T(8,128)(2,1)S(1)} async-done(((bf16[8,32,768]{2,1,0:T(8,128)(2,1)}), bf16[8,32,768]{2,1,0:T(8,128)(2,1)S(1)}, u32[]{:S(2)}, u32[]{:S(2)}) %all-to-all-start) | async-done | bytes 393248 | tf_op jit(solution)/shard_map/all_to_all | solution.py:288
  16.0 6.4 %all-to-all-start.1 = ((bf16[8,48,768]{2,1,0:T(8,128)(2,1)}), bf16[8,48,768]{2,1,0:T(8,128)(2,1)S(1)}, u32[]{:S(2)}, u32[]{:S(2)}) async-start(bf16[8,48,768]{2,1,0:T(8,128)(2,1)} %get-tuple-element.28), calls=%async_computation.1 | async-start | bytes 1179648 | tf_op jit(solution)/shard_map/all_to_all | solution.py:304
  22.3 0.0 collective-permute-done.refs_2_
  22.3 8.9 %kernel_rows.1.refs_1_ = f32[8,16,768]{2,1,0:T(8,128)S(1)} custom-call(bf16[8,32,768]{2,1,0:T(8,128)(2,1)S(1)} %all-to-all-done.refs_0_.refs_3_, bf16[1,48,768]{2,1,0:T(8,128)(2,1)S(1)} %get-tuple-element.27.refs_1_, bf16[1,48,768]{2,1,0:T(8,128)(2,1)S(1)} %bitcast.7), custom_call_target="tpu_custom_call" | custom-call | flops 5637144576 | bytes 3145728 | tf_op jit(solution)/shard_map/kernel_rows/pallas_call | solution.py:189
  31.2 0.6 all-to-all-done.1.refs_4_
  31.9 3.9 %collective-permute-start.1 = (bf16[8,48,768]{2,1,0:T(8,128)(2,1)S(1)}, bf16[8,48,768]{2,1,0:T(8,128)(2,1)S(1)}, u32[]{:S(2)}, u32[]{:S(2)}) collective-permute-start(bf16[8,48,768]{2,1,0:T(8,128)(2,1)S(1)} %all-to-all-done.1.refs_4_), channel_id=1, source_target_pairs={{0,8},{8,0},{16,24},{24,16},{32,40},{40,32},{48,56},{56,48},{64,72... | collective-permute-start | bytes 1769480 | tf_op jit(solution)/shard_map/ppermute | solution.py:314
  35.8 1.6 %collective-permute-done.1.refs_5_ = bf16[8,48,768]{2,1,0:T(8,128)(2,1)S(1)} collective-permute-done((bf16[8,48,768]{2,1,0:T(8,128)(2,1)S(1)}, bf16[8,48,768]{2,1,0:T(8,128)(2,1)S(1)}, u32[]{:S(2)}, u32[]{:S(2)}) %collective-permute-start.1) | collective-permute-done | bytes 589856 | tf_op jit(solution)/shard_map/ppermute | solution.py:314
  37.4 47.6 %kernel_rows_rest.1 = f32[8,16,768]{2,1,0:T(8,128)S(1)} custom-call(s32[1]{0:T(128)} %bitcast.refs_0_, f32[8,16,768]{2,1,0:T(8,128)S(1)} %kernel_rows.1.refs_1_, bf16[48,768]{1,0:T(8,128)(2,1)S(1)} %collective-permute-done.refs_2_, bf16[8,32,768]{2,1,0:T(8,128)(2,1)S(1)} %all-to-all-done.refs_0_.refs_3_, bf16[8,48,768]{2,1,0:T(8,128)(2,1)S(1)} %all-to-all-done.1.refs_4_, ...), custom_call_target="tpu_custom_call" | custom-call | flops 40265318400 | bytes 3145728 | tf_op jit(solution)/shard_map/kernel_rows_rest/pallas_call | solution.py:189
  85.0 11.2 %all_to_all.20.shares_ref = f32[8,16,768]{2,1,0:T(8,128)S(1)} all-to-all(f32[8,16,768]{2,1,0:T(8,128)S(1)} %kernel_rows_rest.1), channel_id=1, replica_groups=mesh['blk'=16,'rows'=8] {'rows'}, dimensions={0} | all-to-all | bytes 786432 | tf_op jit(solution)/shard_map/all_to_all | solution.py:317
  96.2 1.7 %image_and_slots.1 = (f32[16,768]{1,0:T(8,128)}, f32[128,1,384]{2,1,0:T(1,128)S(1)}) custom-call(f32[8,16,768]{2,1,0:T(8,128)S(1)} %all_to_all.20.shares_ref, f32[16,768]{1,0:T(8,128)S(1)} %get-tuple-element.31.dirs_ref, f32[16,768]{1,0:T(8,128)S(1)} %get-tuple-element.32.ridged_ref, s32[1,768]{1,0:T(1,128)S(1)} %get-tuple-element.33.place_ref), custom_call_target="tpu_custom_call" | custom-call | tf_op jit(solution)/shard_map/image_and_slots/pallas_call | solution.py:318
  97.9 17.1 %all_to_all.21.rows_ref = f32[128,1,384]{2,1,0:T(1,128)S(1)} all-to-all(f32[128,1,384]{2,1,0:T(1,128)S(1)} %get-tuple-element.35), channel_id=1, replica_groups=mesh['blk'=16,'rows'=8] {'blk','rows'}, dimensions={0} | all-to-all | bytes 393216 | tf_op jit(solution)/shard_map/all_to_all | solution.py:327
  115.0 1.2 %fold_products.1 = f32[4,256]{1,0:T(4,128)} custom-call(f32[128,1,384]{2,1,0:T(1,128)S(1)} %all_to_all.21.rows_ref), custom_call_target="tpu_custom_call" | custom-call | tf_op jit(solution)/shard_map/fold_products/pallas_call | solution.py:328
Async XLA Ops:
  2.2 6.9 %copy-start = (bf16[48,768]{1,0:T(8,128)(2,1)S(1)}, bf16[48,768]{1,0:T(8,128)(2,1)}, u32[]{:S(2)}) copy-start(bf16[48,768]{1,0:T(8,128)(2,1)} %get-tuple-element.20.panel_ref) | copy-start | bytes 221188
  2.2 13.7 %all-to-all-start = ((bf16[8,32,768]{2,1,0:T(8,128)(2,1)}), bf16[8,32,768]{2,1,0:T(8,128)(2,1)S(1)}, u32[]{:S(2)}, u32[]{:S(2)}) async-start(bf16[8,32,768]{2,1,0:T(8,128)(2,1)} %get-tuple-element.19), calls=%async_computation | async-start | bytes 786432 | tf_op jit(solution)/shard_map/all_to_all | solution.py:288
  9.2 13.2 %collective-permute-start = (bf16[48,768]{1,0:T(8,128)(2,1)S(1)}, bf16[48,768]{1,0:T(8,128)(2,1)S(1)}, u32[]{:S(2)}, u32[]{:S(2)}) collective-permute-start(bf16[48,768]{1,0:T(8,128)(2,1)S(1)} %copy-done), channel_id=1, source_target_pairs={{0,8},{8,0},{16,24},{24,16},{32,40},{40,32},{48,56},{56,48},{64,72... | collective-permute-start | bytes 221192 | tf_op jit(solution)/shard_map/ppermute | solution.py:289
  16.0 15.9 %all-to-all-start.1 = ((bf16[8,48,768]{2,1,0:T(8,128)(2,1)}), bf16[8,48,768]{2,1,0:T(8,128)(2,1)S(1)}, u32[]{:S(2)}, u32[]{:S(2)}) async-start(bf16[8,48,768]{2,1,0:T(8,128)(2,1)} %get-tuple-element.28), calls=%async_computation.1 | async-start | bytes 1179648 | tf_op jit(solution)/shard_map/all_to_all | solution.py:304
  31.9 5.5 %collective-permute-start.1 = (bf16[8,48,768]{2,1,0:T(8,128)(2,1)S(1)}, bf16[8,48,768]{2,1,0:T(8,128)(2,1)S(1)}, u32[]{:S(2)}, u32[]{:S(2)}) collective-permute-start(bf16[8,48,768]{2,1,0:T(8,128)(2,1)S(1)} %all-to-all-done.1.refs_4_), channel_id=1, source_target_pairs={{0,8},{8,0},{16,24},{24,16},{32,40},{40,32},{48,56},{56,48},{64,72... | collective-permute-start | bytes 1769480 | tf_op jit(solution)/shard_map/ppermute | solution.py:314

commit v6 on v5

--- a/solution.py
+++ b/solution.py
@@ -205,14 +205,13 @@
     )(*([own, before, near] if skip else []), rows_of, columns_of, more_columns)
 
 
-def panel_body(points_ref, dirs_ref, panel_ref, to_rows_ref):
+def rows_body(points_ref, to_rows_ref):
     points = points_ref[...]
-    panel_ref[...] = jnp.concatenate([points, dirs_ref[...].astype(jnp.bfloat16)], axis=0)
     for device in range(to_rows_ref.shape[0]):
         to_rows_ref[device] = points
 
 
-def place_body(ids_ref, dirs_ref, ridge_ref, panel_ref, place_ref, copy_ref, ridged_ref, own_ref, to_pairs_ref):
+def place_body(ids_ref, points_ref, dirs_ref, ridge_ref, place_ref, copy_ref, ridged_ref, own_ref, to_pairs_ref):
     ids = ids_ref[...]
     samples = ids.shape[1]
     named = ids.astype(jnp.float32)
@@ -230,9 +229,10 @@
     diagonal = lax.broadcasted_iota(jnp.int32, square, 0) == lax.broadcasted_iota(jnp.int32, square, 1)
     copy_ref[...] = dirs
     ridged_ref[...] = jnp.sum(jnp.where(diagonal, ridge_ref[...], 0.0), axis=1, keepdims=True) * dirs
-    own_ref[0] = panel_ref[...]
+    panel = jnp.concatenate([points_ref[...], dirs.astype(jnp.bfloat16)], axis=0)
+    own_ref[0] = panel
     for device in range(to_pairs_ref.shape[0]):
-        to_pairs_ref[device] = panel_ref[...]
+        to_pairs_ref[device] = panel
 
 
 def scatter_body(devices, shares_ref, dirs_ref, ridged_ref, place_ref, image_ref, send_ref):
@@ -277,27 +277,24 @@
     pairs = blk_count // 2
     swap = [(place, place ^ 1) for place in range(blk_count)]
     dirs = search_vectors.T
-    panel, to_rows = pl.pallas_call(
-        panel_body,
-        out_shape=[
-            jax.ShapeDtypeStruct((FEAT + RIDGE, samples), jnp.bfloat16),
-            jax.ShapeDtypeStruct((row_count, FEAT, samples), jnp.bfloat16),
-        ],
-        name="panels",
-    )(observation_points.T, dirs)
+    points = observation_points.T
+    to_rows = pl.pallas_call(
+        rows_body, out_shape=jax.ShapeDtypeStruct((row_count, FEAT, samples), jnp.bfloat16), name="rows_to_send"
+    )(points)
     rows_of = lax.all_to_all(to_rows, "rows", 0, 0, tiled=True)
-    partner = lax.ppermute(panel, "blk", swap)
+    panel_shape = (FEAT + RIDGE, samples)
     place, dirs, ridged, own_panel, to_pairs = pl.pallas_call(
         place_body,
         out_shape=[
             pltpu.VMEM((1, samples), jnp.int32),
             pltpu.VMEM(dirs.shape, jnp.float32),
             pltpu.VMEM(dirs.shape, jnp.float32),
-            pltpu.VMEM((1, *panel.shape), jnp.bfloat16),
-            jax.ShapeDtypeStruct((pairs, *panel.shape), jnp.bfloat16),
+            pltpu.VMEM((1, *panel_shape), jnp.bfloat16),
+            jax.ShapeDtypeStruct((pairs, *panel_shape), jnp.bfloat16),
         ],
         name="places",
-    )(holdout_group.T, dirs, shrinkage_levels[None], panel)
+    )(holdout_group.T, points, dirs, shrinkage_levels[None])
+    partner = lax.ppermute(own_panel, "blk", swap)
     rows_of, to_pairs, own_panel, place, dirs, ridged = lax.optimization_barrier(
         (rows_of, to_pairs, own_panel, place, dirs, ridged)
     )
@@ -309,11 +306,11 @@
         tiled=True,
         axis_index_groups=[[2 * pair + core for pair in range(pairs)] for core in range(2)],
     )
-    near = apply_kernel(rows_of, own_panel, partner[None])
+    near = apply_kernel(rows_of, own_panel, partner)
     near, columns_of = lax.optimization_barrier((near, columns_of))
     more_columns = lax.ppermute(columns_of, "blk", swap)
     own = (lax.axis_index("blk") // 2).astype(jnp.int32)[None]
-    shares = apply_kernel(rows_of, columns_of, more_columns, own, near, partner)
+    shares = apply_kernel(rows_of, columns_of, more_columns, own, near, partner[0])
     shares = lax.all_to_all(shares, "rows", 0, 0, tiled=True)
     image, send = pl.pallas_call(
         functools.partial(scatter_body, devices),

time: 117 us -> 116 us (level)
  no operation moved by 1% of the time
where the time goes in v6:
time: 116 us
  Pallas kernels  62.8 us (54%)
  blocking collectives  28.3 us (24%)
  starting transfers between devices  18 us (16%)
  waiting for transfers between devices  6.19 us (5%)
    pallas_call x2, Pallas kernels, apply_kernel(): pl.pallas_call(functools.partial(apply_body, skip), out_shape=jax.ShapeDt...  56.5 us
    all_to_all x1, blocking collectives, body(): received = lax.all_to_all(send, ('blk', 'rows'), 0, 0, tiled=True)  17.1 us
    all_to_all x1, blocking collectives, body(): shares = lax.all_to_all(shares, 'rows', 0, 0, tiled=True)  11.2 us
    all_to_all x1, starting transfers between devices, body(): rows_of = lax.all_to_all(to_rows, 'rows', 0, 0, tiled=True)  6.79 us
    all_to_all x1, starting transfers between devices, body(): lax.all_to_all(to_pairs, 'blk', 0, 0, tiled=True, axis_index_groups=[[2 *...  6.36 us
    all_to_all x1, waiting for transfers between devices, body(): rows_of = lax.all_to_all(to_rows, 'rows', 0, 0, tiled=True)  3.92 us
    ppermute x1, starting transfers between devices, body(): more_columns = lax.ppermute(columns_of, 'blk', swap)  3.91 us
  transfers between devices with their start and end apart: 4, of which 3 were waited for; matrix products, arithmetic and copies ran while one was open for 0% of the time, Pallas kernels for 9%

profile of v6, /device:TPU:1, one launch (start us, length us, event | category | flops | bytes accessed | tf_op | source)
XLA Modules:
  0.0 116.0 jit_solution(3489427000609619767)
XLA Ops:
  0.6 1.6 %rows_to_send.1 = bf16[8,32,768]{2,1,0:T(8,128)(2,1)} custom-call(bf16[32,768]{1,0:T(8,128)(2,1)} %bitcast.8), custom_call_target="tpu_custom_call" | custom-call | tf_op jit(solution)/shard_map/rows_to_send/pallas_call | solution.py:281
  2.2 6.8 %all-to-all-start = ((bf16[8,32,768]{2,1,0:T(8,128)(2,1)}), bf16[8,32,768]{2,1,0:T(8,128)(2,1)S(1)}, u32[]{:S(2)}, u32[]{:S(2)}) async-start(bf16[8,32,768]{2,1,0:T(8,128)(2,1)} %rows_to_send.1), calls=%async_computation | async-start | bytes 786432 | tf_op jit(solution)/shard_map/all_to_all | solution.py:284
  9.0 1.9 %places.1 = (s32[1,768]{1,0:T(1,128)S(1)}, f32[16,768]{1,0:T(8,128)S(1)}, f32[16,768]{1,0:T(8,128)S(1)}, bf16[1,48,768]{2,1,0:T(8,128)(2,1)S(1)}, bf16[8,48,768]{2,1,0:T(8,128)(2,1)}) custom-call(s32[1,768]{1,0:T(1,128)} %bitcast.11, bf16[32,768]{1,0:T(8,128)(2,1)} %bitcast.9, f32[16,768]{1,0:T(8,128)} %bitcast.10, f32[1,16]{1,0:T(1,128)} %bitcast.12), custom_call_target="tpu_custom_call" | custom-call | tf_op jit(solution)/shard_map/places/pallas_call | solution.py:286
  10.9 1.0 collective-permute-start
  11.9 3.9 %all-to-all-done.refs_0_.refs_3_ = bf16[8,32,768]{2,1,0:T(8,128)(2,1)S(1)} async-done(((bf16[8,32,768]{2,1,0:T(8,128)(2,1)}), bf16[8,32,768]{2,1,0:T(8,128)(2,1)S(1)}, u32[]{:S(2)}, u32[]{:S(2)}) %all-to-all-start) | async-done | bytes 393248 | tf_op jit(solution)/shard_map/all_to_all | solution.py:284
  15.8 6.4 %all-to-all-start.1 = ((bf16[8,48,768]{2,1,0:T(8,128)(2,1)}), bf16[8,48,768]{2,1,0:T(8,128)(2,1)S(1)}, u32[]{:S(2)}, u32[]{:S(2)}) async-start(bf16[8,48,768]{2,1,0:T(8,128)(2,1)} %get-tuple-element.24), calls=%async_computation.1 | async-start | bytes 1179648 | tf_op jit(solution)/shard_map/all_to_all | solution.py:301
  22.1 0.0 collective-permute-done.refs_2_
  22.2 8.9 %kernel_rows.1.refs_1_ = f32[8,16,768]{2,1,0:T(8,128)S(1)} custom-call(bf16[8,32,768]{2,1,0:T(8,128)(2,1)S(1)} %all-to-all-done.refs_0_.refs_3_, bf16[1,48,768]{2,1,0:T(8,128)(2,1)S(1)} %get-tuple-element.23.refs_1_, bf16[1,48,768]{2,1,0:T(8,128)(2,1)S(1)} %collective-permute-done.refs_2_), custom_call_target="tpu_custom_call" | custom-call | flops 5637144576 | bytes 3145728 | tf_op jit(solution)/shard_map/kernel_rows/pallas_call | solution.py:189
  31.0 0.6 all-to-all-done.1.refs_4_
  31.7 3.9 %collective-permute-start.1 = (bf16[8,48,768]{2,1,0:T(8,128)(2,1)S(1)}, bf16[8,48,768]{2,1,0:T(8,128)(2,1)S(1)}, u32[]{:S(2)}, u32[]{:S(2)}) collective-permute-start(bf16[8,48,768]{2,1,0:T(8,128)(2,1)S(1)} %all-to-all-done.1.refs_4_), channel_id=1, source_target_pairs={{0,8},{8,0},{16,24},{24,16},{32,40},{40,32},{48,56},{56,48},{64,72... | collective-permute-start | bytes 1769480 | tf_op jit(solution)/shard_map/ppermute | solution.py:311
  35.6 1.6 %collective-permute-done.1.refs_5_ = bf16[8,48,768]{2,1,0:T(8,128)(2,1)S(1)} collective-permute-done((bf16[8,48,768]{2,1,0:T(8,128)(2,1)S(1)}, bf16[8,48,768]{2,1,0:T(8,128)(2,1)S(1)}, u32[]{:S(2)}, u32[]{:S(2)}) %collective-permute-start.1) | collective-permute-done | bytes 589856 | tf_op jit(solution)/shard_map/ppermute | solution.py:311
  37.2 47.6 %kernel_rows_rest.1 = f32[8,16,768]{2,1,0:T(8,128)S(1)} custom-call(s32[1]{0:T(128)} %bitcast.refs_0_, f32[8,16,768]{2,1,0:T(8,128)S(1)} %kernel_rows.1.refs_1_, bf16[48,768]{1,0:T(8,128)(2,1)S(1)} %bitcast.7, bf16[8,32,768]{2,1,0:T(8,128)(2,1)S(1)} %all-to-all-done.refs_0_.refs_3_, bf16[8,48,768]{2,1,0:T(8,128)(2,1)S(1)} %all-to-all-done.1.refs_4_, ...), custom_call_target="tpu_custom_call" | custom-call | flops 40265318400 | bytes 3145728 | tf_op jit(solution)/shard_map/kernel_rows_rest/pallas_call | solution.py:189
  84.8 11.2 %all_to_all.20.shares_ref = f32[8,16,768]{2,1,0:T(8,128)S(1)} all-to-all(f32[8,16,768]{2,1,0:T(8,128)S(1)} %kernel_rows_rest.1), channel_id=1, replica_groups=mesh['blk'=16,'rows'=8] {'rows'}, dimensions={0} | all-to-all | bytes 786432 | tf_op jit(solution)/shard_map/all_to_all | solution.py:314
  96.0 1.7 %image_and_slots.1 = (f32[16,768]{1,0:T(8,128)}, f32[128,1,384]{2,1,0:T(1,128)S(1)}) custom-call(f32[8,16,768]{2,1,0:T(8,128)S(1)} %all_to_all.20.shares_ref, f32[16,768]{1,0:T(8,128)S(1)} %get-tuple-element.27.dirs_ref, f32[16,768]{1,0:T(8,128)S(1)} %get-tuple-element.28.ridged_ref, s32[1,768]{1,0:T(1,128)S(1)} %get-tuple-element.29.place_ref), custom_call_target="tpu_custom_call" | custom-call | tf_op jit(solution)/shard_map/image_and_slots/pallas_call | solution.py:315
  97.7 17.1 %all_to_all.21.rows_ref = f32[128,1,384]{2,1,0:T(1,128)S(1)} all-to-all(f32[128,1,384]{2,1,0:T(1,128)S(1)} %get-tuple-element.31), channel_id=1, replica_groups=mesh['blk'=16,'rows'=8] {'blk','rows'}, dimensions={0} | all-to-all | bytes 393216 | tf_op jit(solution)/shard_map/all_to_all | solution.py:324
  114.8 1.2 %fold_products.1 = f32[4,256]{1,0:T(4,128)} custom-call(f32[128,1,384]{2,1,0:T(1,128)S(1)} %all_to_all.21.rows_ref), custom_call_target="tpu_custom_call" | custom-call | tf_op jit(solution)/shard_map/fold_products/pallas_call | solution.py:325
Async XLA Ops:
  2.2 13.6 %all-to-all-start = ((bf16[8,32,768]{2,1,0:T(8,128)(2,1)}), bf16[8,32,768]{2,1,0:T(8,128)(2,1)S(1)}, u32[]{:S(2)}, u32[]{:S(2)}) async-start(bf16[8,32,768]{2,1,0:T(8,128)(2,1)} %rows_to_send.1), calls=%async_computation | async-start | bytes 786432 | tf_op jit(solution)/shard_map/all_to_all | solution.py:284
  10.9 11.2 %collective-permute-start = (bf16[1,48,768]{2,1,0:T(8,128)(2,1)S(1)}, bf16[1,48,768]{2,1,0:T(8,128)(2,1)S(1)}, u32[]{:S(2)}, u32[]{:S(2)}) collective-permute-start(bf16[1,48,768]{2,1,0:T(8,128)(2,1)S(1)} %get-tuple-element.23.refs_1_), channel_id=1, source_target_pairs={{0,8},{8,0},{16,24},{24,16},{32,40},{40,32},{48,56},{56,48},{64,72... | collective-permute-start | bytes 221192 | tf_op jit(solution)/shard_map/ppermute | solution.py:297
  15.8 15.9 %all-to-all-start.1 = ((bf16[8,48,768]{2,1,0:T(8,128)(2,1)}), bf16[8,48,768]{2,1,0:T(8,128)(2,1)S(1)}, u32[]{:S(2)}, u32[]{:S(2)}) async-start(bf16[8,48,768]{2,1,0:T(8,128)(2,1)} %get-tuple-element.24), calls=%async_computation.1 | async-start | bytes 1179648 | tf_op jit(solution)/shard_map/all_to_all | solution.py:301
  31.7 5.5 %collective-permute-start.1 = (bf16[8,48,768]{2,1,0:T(8,128)(2,1)S(1)}, bf16[8,48,768]{2,1,0:T(8,128)(2,1)S(1)}, u32[]{:S(2)}, u32[]{:S(2)}) collective-permute-start(bf16[8,48,768]{2,1,0:T(8,128)(2,1)S(1)} %all-to-all-done.1.refs_4_), channel_id=1, source_target_pairs={{0,8},{8,0},{16,24},{24,16},{32,40},{40,32},{48,56},{56,48},{64,72... | collective-permute-start | bytes 1769480 | tf_op jit(solution)/shard_map/ppermute | solution.py:311
